TPU v7x, 128 devices: a whole 4x4x4 slice. The times are simulated.
128 devices in a mesh: ctx: 32 (over y, z, core), ch: 4 (over x).
Axes of the slice: x: 4, y: 4, z: 4, core: 2. Of those that a mesh axis runs over, the one named last changes fastest.
Arguments:
- branches: bfloat16 [16384, 3, 4096], P('ctx', None, 'ch'), may hold values from -6 to 6
- short_kernel: float32 [3, 3, 4096], P(None, None, 'ch'), may hold values from -3 to 3
- long_filter: float32 [16384, 4096], P('ctx', 'ch'), may hold values from -2 to 2
- skip_gain: float32 [4096], P('ch'), may hold values from -4 to 4
- out_weight: bfloat16 [4096, 4096], P('ch'), may hold values from -0.09375 to 0.09375
Outputs:
- mixed: bfloat16 [16384, 4096], P('ctx', 'ch')
All inputs are finite; a program needn't handle non-finite values.
Results may differ from a plain program's by a relative error of at most 0.02.
Values may be sent and summed in bfloat16 or wider, within the bound.
A program may use at most 256 MiB of HBM per device.

v0:
```python
import math

import jax
import jax.numpy as jnp
from jax import lax
from jax.sharding import PartitionSpec as P

highest = lax.Precision.HIGHEST


def passed_along(array, axis, by):
    count = lax.axis_size(axis)
    pairs = [(i, i + by) for i in range(count) if 0 <= i + by < count]
    return lax.ppermute(array, axis, pairs)


def shortened(array):

    def short(part):
        return part.astype(jnp.bfloat16) if part.dtype == jnp.float32 else part

    return jax.tree.map(short, array)


def contract(form, table, values):
    return jnp.einsum(form, table, values, precision=highest)


def split_length(length):
    best = 1
    for factor in range(1, math.isqrt(length) + 1):
        if length % factor == 0:
            best = factor
    return best


def phase_table(first, second, period):
    phase = first * second % period
    angle = 2.0 * math.pi / period * phase.astype(jnp.float32)
    return (jnp.cos(angle), jnp.sin(angle))


def column_real(table_cos, table_sin, values):
    return (contract("en,nmc->emc", table_cos, values), -contract("en,nmc->emc", table_sin, values))


def local_forward(real_part, imag_part, classes, length_fft):
    count_e, rows, chans = real_part.shape
    first_len = split_length(rows)
    second_len = rows // first_len
    places = jnp.arange(rows, dtype=jnp.int32)
    tw_cos, tw_sin = phase_table(classes[:, None], places[None, :], length_fft)
    tw_cos = tw_cos[:, :, None]
    tw_sin = tw_sin[:, :, None]
    real_part, imag_part = (
        real_part * tw_cos + imag_part * tw_sin,
        imag_part * tw_cos - real_part * tw_sin,
    )
    real_part = real_part.reshape(count_e, first_len, second_len, chans)
    imag_part = imag_part.reshape(count_e, first_len, second_len, chans)
    first_ids = jnp.arange(first_len, dtype=jnp.int32)
    second_ids = jnp.arange(second_len, dtype=jnp.int32)
    fa_cos, fa_sin = phase_table(first_ids[:, None], first_ids[None, :], first_len)
    step_real = contract("pa,eabc->epbc", fa_cos, real_part) + contract(
        "pa,eabc->epbc", fa_sin, imag_part
    )
    step_imag = contract("pa,eabc->epbc", fa_cos, imag_part) - contract(
        "pa,eabc->epbc", fa_sin, real_part
    )
    mid_cos, mid_sin = phase_table(first_ids[:, None], second_ids[None, :], rows)
    mid_cos = mid_cos[None, :, :, None]
    mid_sin = mid_sin[None, :, :, None]
    step_real, step_imag = (
        step_real * mid_cos + step_imag * mid_sin,
        step_imag * mid_cos - step_real * mid_sin,
    )
    fb_cos, fb_sin = phase_table(second_ids[:, None], second_ids[None, :], second_len)
    out_real = contract("qb,epbc->eqpc", fb_cos, step_real) + contract(
        "qb,epbc->eqpc", fb_sin, step_imag
    )
    out_imag = contract("qb,epbc->eqpc", fb_cos, step_imag) - contract(
        "qb,epbc->eqpc", fb_sin, step_real
    )
    return (out_real.reshape(count_e, rows, chans), out_imag.reshape(count_e, rows, chans))


def local_inverse(real_part, imag_part, classes, length_fft):
    count_e, rows, chans = real_part.shape
    first_len = split_length(rows)
    second_len = rows // first_len
    first_ids = jnp.arange(first_len, dtype=jnp.int32)
    second_ids = jnp.arange(second_len, dtype=jnp.int32)
    real_part = real_part.reshape(count_e, second_len, first_len, chans)
    imag_part = imag_part.reshape(count_e, second_len, first_len, chans)
    fb_cos, fb_sin = phase_table(second_ids[:, None], second_ids[None, :], second_len)
    step_real = contract("bq,eqpc->ebpc", fb_cos, real_part) - contract(
        "bq,eqpc->ebpc", fb_sin, imag_part
    )
    step_imag = contract("bq,eqpc->ebpc", fb_cos, imag_part) + contract(
        "bq,eqpc->ebpc", fb_sin, real_part
    )
    mid_cos, mid_sin = phase_table(second_ids[:, None], first_ids[None, :], rows)
    mid_cos = mid_cos[None, :, :, None]
    mid_sin = mid_sin[None, :, :, None]
    step_real, step_imag = (
        step_real * mid_cos - step_imag * mid_sin,
        step_imag * mid_cos + step_real * mid_sin,
    )
    fa_cos, fa_sin = phase_table(first_ids[:, None], first_ids[None, :], first_len)
    out_real = contract("ap,ebpc->eabc", fa_cos, step_real) - contract(
        "ap,ebpc->eabc", fa_sin, step_imag
    )
    out_imag = contract("ap,ebpc->eabc", fa_cos, step_imag) + contract(
        "ap,ebpc->eabc", fa_sin, step_real
    )
    out_real = out_real.reshape(count_e, rows, chans)
    out_imag = out_imag.reshape(count_e, rows, chans)
    places = jnp.arange(rows, dtype=jnp.int32)
    tw_cos, tw_sin = phase_table(classes[:, None], places[None, :], length_fft)
    tw_cos = tw_cos[:, :, None]
    tw_sin = tw_sin[:, :, None]
    return (out_real * tw_cos - out_imag * tw_sin, out_imag * tw_cos + out_real * tw_sin)


def inverse_column(table_cos, table_sin, real_part, imag_part):
    return contract("ne,emc->nmc", table_cos, real_part) - contract(
        "ne,emc->nmc", table_sin, imag_part
    )


def on_device(branches, short_kernel, long_filter, skip_gain, out_weight):
    ctx_count = lax.axis_size("ctx")
    device_index = lax.axis_index("ctx")
    local_rows = branches.shape[0]
    chans = branches.shape[2]
    taps = short_kernel.shape[0]
    length_fft = 2 * ctx_count * local_rows
    doubled = 2 * ctx_count
    earlier = passed_along(branches[local_rows - (taps - 1) :], "ctx", 1)
    extended = jnp.concatenate([earlier, branches], axis=0).astype(jnp.float32)
    featured = jnp.zeros((local_rows, 3, chans), jnp.float32)
    for offset in range(taps):
        featured = (
            featured
            + short_kernel[offset][None, :, :]
            * extended[taps - 1 - offset : taps - 1 - offset + local_rows]
        )
    query = featured[:, 0]
    driven = featured[:, 1] * featured[:, 2]
    signals = jnp.stack([driven, long_filter])
    pieces = lax.all_to_all(
        signals[:, None].astype(jnp.bfloat16), "ctx", split_axis=2, concat_axis=1, tiled=True
    ).astype(jnp.float32)
    slot_ids = jnp.arange(ctx_count, dtype=jnp.int32)
    all_classes = jnp.concatenate(
        [slot_ids, jnp.where(slot_ids == 0, ctx_count, doubled - slot_ids)]
    )
    own_classes = jnp.stack(
        [device_index, jnp.where(device_index == 0, ctx_count, doubled - device_index)]
    )
    block_ids = jnp.arange(ctx_count, dtype=jnp.int32)
    fwd_cos, fwd_sin = phase_table(all_classes[:, None], block_ids[None, :], doubled)
    slice_rows = pieces.shape[2]
    slice_chans = pieces.shape[3]
    driven_cols = column_real(fwd_cos, fwd_sin, pieces[0])
    filter_cols = column_real(fwd_cos, fwd_sin, pieces[1])
    stacked = jnp.stack([jnp.stack(driven_cols), jnp.stack(filter_cols)])
    stacked = stacked.reshape(2, 2, 2, ctx_count, slice_rows, slice_chans)
    stacked = (
        lax.all_to_all(shortened(stacked), "ctx", split_axis=3, concat_axis=4, tiled=True)
        .astype(stacked.dtype)
        .reshape(2, 2, 2, local_rows, slice_chans)
    )
    driven_spec = local_forward(stacked[0, 0], stacked[0, 1], own_classes, length_fft)
    filter_spec = local_forward(stacked[1, 0], stacked[1, 1], own_classes, length_fft)
    prod_real = driven_spec[0] * filter_spec[0] - driven_spec[1] * filter_spec[1]
    prod_imag = driven_spec[0] * filter_spec[1] + driven_spec[1] * filter_spec[0]
    wave_real, wave_imag = local_inverse(prod_real, prod_imag, own_classes, length_fft)
    inv_cos, inv_sin = phase_table(block_ids[:, None], all_classes[None, :], doubled)
    waves = jnp.stack([wave_real, wave_imag])[:, :, None]
    moved = (
        lax.all_to_all(shortened(waves), "ctx", split_axis=3, concat_axis=2, tiled=True)
        .astype(waves.dtype)
        .reshape(2, doubled, local_rows // ctx_count, chans)
    )
    real_rows = inverse_column(inv_cos, inv_sin, moved[0], moved[1])
    long_conv = (
        lax.all_to_all(shortened(real_rows), "ctx", split_axis=0, concat_axis=1, tiled=True).astype(
            real_rows.dtype
        )[0]
        / length_fft
    )
    gated = (query * (long_conv + skip_gain * driven)).astype(jnp.bfloat16)
    terms = jnp.dot(gated, out_weight, preferred_element_type=jnp.float32)
    summed = lax.psum_scatter(terms.astype(jnp.bfloat16), "ch", scatter_dimension=1, tiled=True)
    return summed


def solution(mesh):
    placed = (P("ctx", None, "ch"), P(None, None, "ch"), P("ctx", "ch"), P("ch"), P("ch", None))
    return jax.shard_map(
        on_device, mesh=mesh, in_specs=placed, out_specs=P("ctx", "ch"), check_vma=False
    )
```

profile of v0, /device:TPU:1, one launch (start us, length us, event | category | flops | bytes accessed | tf_op | source)
XLA Modules:
  0.0 615.4 jit_solution(4479536535698865060)
XLA Ops:
  24.0 7.8 %all-to-all-start = ((bf16[2,1,512,1024]{3,0,1,2:T(2,128)(2,1)}), bf16[2,1,512,1024]{3,0,1,2:T(2,128)(2,1)S(1)}, u32[]{:S(2)}, u32[]{:S(2)}) async-start(bf16[2,1,512,1024]{3,0,1,2:T(2,128)(2,1)} %copy.93), calls=%async_computation | async-start | bytes 4194304 | tf_op jit(solution)/shard_map/all_to_all | solution.py:151
  32.0 28.1 %all-to-all-done = bf16[2,1,512,1024]{3,0,1,2:T(2,128)(2,1)S(1)} async-done(((bf16[2,1,512,1024]{3,0,1,2:T(2,128)(2,1)}), bf16[2,1,512,1024]{3,0,1,2:T(2,128)(2,1)S(1)}, u32[]{:S(2)}, u32[]{:S(2)}) %all-to-all-start) | async-done | bytes 2097184 | tf_op jit(solution)/shard_map/all_to_all | solution.py:151
  78.9 11.3 %copy.104 = bf16[2,2,2,32,16,1024]{5,4,2,1,0,3:T(8,128)(2,1)} copy(bf16[2,2,2,32,16,1024]{5,3,4,2,1,0:T(8,128)(2,1)} %maximum_maximum_fusion) | data formatting | bytes 16777216 | tf_op jit(solution)/shard_map/stack | solution.py:167
  96.3 106.2 %all-to-all-done.1 = bf16[2,2,2,32,16,1024]{5,4,2,1,0,3:T(8,128)(2,1)} async-done(((bf16[2,2,2,32,16,1024]{5,4,2,1,0,3:T(8,128)(2,1)}), bf16[2,2,2,32,16,1024]{5,4,2,1,0,3:T(8,128)(2,1)}, u32[]{:S(2)}, u32[]{:S(2)}) %all-to-all-start.1) | async-done | bytes 8388640 | tf_op jit(solution)/shard_map/all_to_all | solution.py:170
  202.5 8.6 %copy.105 = bf16[2,2,2,32,16,1024]{5,4,3,2,1,0:T(8,128)(2,1)} copy(bf16[2,2,2,32,16,1024]{5,4,2,1,0,3:T(8,128)(2,1)} %all-to-all-done.1) | data formatting | bytes 16777216 | tf_op jit(solution)/shard_map/all_to_all | solution.py:170
  211.0 11.3 %bitcast_convert_fusion = f32[2,2,2,512,1024]{4,3,2,1,0:T(8,128)} fusion(bf16[2,2,2,32,16,1024]{5,4,3,2,1,0:T(8,128)(2,1)} %copy.105), kind=kLoop, calls=%fused_computation.1 | loop fusion | flops 4194304 | bytes 25165824 | tf_op jit(solution)/shard_map/convert_element_type | solution.py:171
  222.3 12.4 %fusion.359 = (f32[1,1,2,512,1024]{4,3,2,1,0:T(8,128)}, f32[1,1,2,512,1024]{4,3,2,1,0:T(8,128)}, f32[1,1,2,512,1024]{4,3,2,1,0:T(8,128)}, f32[1,1,2,512,1024]{4,3,2,1,0:T(8,128)}) fusion(f32[2,2,2,512,1024]{4,3,2,1,0:T(8,128)} %bitcast_convert_fusion), kind=kLoop, calls=%fused_computation.382 | loop fusion | bytes 33554432 | tf_op jit(solution)/shard_map/slice | solution.py:175
  234.7 7.5 %multiply_add_fusion.1 = (f32[2,16,32,1024]{3,2,1,0:T(8,128)S(1)}, f32[2,16,32,1024]{3,2,1,0:T(8,128)S(1)}, f32[2,16,32,1024]{3,2,1,0:T(8,128)S(1)}, f32[2,16,32,1024]{3,2,1,0:T(8,128)S(1)}) fusion(f32[2,16,32,1024]{3,2,1,0:T(8,128)} %bitcast.207, f32[2,16,32,1024]{3,2,1,0:T(8,128)} %bitcast.208, f32[2,16,32]{2,1,0:T(8,128)S(1)} %get-tuple-element.35, ...), kind=kLoop, calls=%fused_computation.42 | loop fusion | flops 12582912 | bytes 33562624 | tf_op jit(solution)/shard_map/add | solution.py:56
  242.2 7.8 %fusion.48 = f32[2,32,1024,16]{2,3,1,0:T(8,128)S(1)} fusion(f32[2,16,32,1024]{3,2,1,0:T(8,128)S(1)} %get-tuple-element.32), kind=kOutput, calls=%fused_computation.79 | convolution fusion | flops 201330176 | bytes 8388608 | tf_op jit(solution)/shard_map/pa,eabc->epbc/dot_general | solution.py:26
  250.0 7.9 %fusion.50 = f32[2,32,1024,16]{2,3,1,0:T(8,128)S(1)} fusion(f32[2,16,32,1024]{3,2,1,0:T(8,128)S(1)} %get-tuple-element.32), kind=kOutput, calls=%fused_computation.81 | convolution fusion | flops 201330176 | bytes 8388608 | tf_op jit(solution)/shard_map/pa,eabc->epbc/dot_general | solution.py:26
  257.9 7.7 %fusion.34 = f32[2,32,1024,16]{2,3,1,0:T(8,128)S(1)} fusion(f32[2,16,32,1024]{3,2,1,0:T(8,128)S(1)} %get-tuple-element.14), kind=kOutput, calls=%fused_computation.65 | convolution fusion | flops 201330176 | bytes 8388608 | tf_op jit(solution)/shard_map/pa,eabc->epbc/dot_general | solution.py:26
  265.6 7.0 %fusion.32 = f32[2,32,1024,16]{2,3,1,0:T(8,128)} fusion(f32[2,16,32,1024]{3,2,1,0:T(8,128)S(1)} %get-tuple-element.14), kind=kOutput, calls=%fused_computation.63 | convolution fusion | flops 201330176 | bytes 8388608 | tf_op jit(solution)/shard_map/pa,eabc->epbc/dot_general | solution.py:26
  272.6 7.6 %fusion.59 = f32[2,32,1024,16]{2,3,1,0:T(8,128)} fusion(f32[2,32,1024,16]{2,3,1,0:T(8,128)S(1)} %fusion.48, f32[2,16,32,1024]{3,2,1,0:T(8,128)S(1)} %get-tuple-element.33), kind=kOutput, calls=%fused_computation.89 | convolution fusion | flops 202378752 | bytes 12582912 | tf_op jit(solution)/shard_map/pa,eabc->epbc/dot_general | solution.py:26
  280.2 7.4 %fusion.56 = f32[2,32,1024,16]{2,3,1,0:T(8,128)} fusion(f32[2,32,1024,16]{2,3,1,0:T(8,128)S(1)} %fusion.50, f32[2,16,32,1024]{3,2,1,0:T(8,128)S(1)} %get-tuple-element.33), kind=kOutput, calls=%fused_computation.88 | convolution fusion | flops 202378752 | bytes 12582912 | tf_op jit(solution)/shard_map/pa,eabc->epbc/dot_general | solution.py:26
  287.6 7.4 %fusion.68 = f32[2,32,1024,16]{2,3,1,0:T(8,128)} fusion(f32[2,32,1024,16]{2,3,1,0:T(8,128)S(1)} %fusion.34, f32[2,16,32,1024]{3,2,1,0:T(8,128)S(1)} %get-tuple-element.13), kind=kOutput, calls=%fused_computation.92 | convolution fusion | flops 202378752 | bytes 12582912 | tf_op jit(solution)/shard_map/pa,eabc->epbc/dot_general | solution.py:26
  295.1 15.6 %fusion.12 = (f32[2,16,32,1024]{3,1,2,0:T(8,128)S(1)}, f32[2,16,32,1024]{3,1,2,0:T(8,128)}, f32[2,16,32,1024]{3,1,2,0:T(8,128)}, f32[2,16,32,1024]{3,1,2,0:T(8,128)S(1)}) fusion(f32[2,32,1024,16]{2,3,1,0:T(8,128)} %fusion.68, f32[16,32]{0,1:T(8,128)S(1)} %get-tuple-element.38, f32[16,32]{0,1:T(8,128)S(1)} %get-tuple-element.39, ...), kind=kOutput, calls=%fused_computation.25 | convolution fusion | flops 214961664 | bytes 37752832 | tf_op jit(solution)/shard_map/pa,eabc->epbc/dot_general | solution.py:26
  310.7 9.2 %fusion.26 = f32[2,16,1024,32]{2,3,1,0:T(8,128)S(1)} fusion(f32[2,16,32,1024]{3,1,2,0:T(8,128)} %get-tuple-element.12), kind=kOutput, calls=%fused_computation.57 | convolution fusion | flops 402667520 | bytes 8388608 | tf_op jit(solution)/shard_map/qb,epbc->eqpc/dot_general | solution.py:26
  320.0 8.0 %fusion.24 = f32[2,16,1024,32]{2,3,1,0:T(8,128)S(1)} fusion(f32[2,16,32,1024]{3,1,2,0:T(8,128)S(1)} %copy-done.2), kind=kOutput, calls=%fused_computation.55 | convolution fusion | flops 402667520 | bytes 8388608 | tf_op jit(solution)/shard_map/qb,epbc->eqpc/dot_general | solution.py:26
  328.0 8.4 %fusion.42 = f32[2,16,1024,32]{2,3,1,0:T(8,128)S(1)} fusion(f32[2,16,32,1024]{3,1,2,0:T(8,128)S(1)} %copy-done.1), kind=kOutput, calls=%fused_computation.73 | convolution fusion | flops 402667520 | bytes 8388608 | tf_op jit(solution)/shard_map/qb,epbc->eqpc/dot_general | solution.py:26
  336.5 7.3 %fusion.40 = f32[2,16,1024,32]{2,3,1,0:T(8,128)} fusion(f32[2,16,32,1024]{3,1,2,0:T(8,128)S(1)} %copy-done.1), kind=kOutput, calls=%fused_computation.71 | convolution fusion | flops 402667520 | bytes 8388608 | tf_op jit(solution)/shard_map/qb,epbc->eqpc/dot_general | solution.py:26
  343.8 7.8 %fusion.74 = f32[2,16,1024,32]{2,3,1,0:T(8,128)} fusion(f32[2,16,1024,32]{2,3,1,0:T(8,128)S(1)} %fusion.26, f32[2,16,32,1024]{3,1,2,0:T(8,128)S(1)} %get-tuple-element.11), kind=kOutput, calls=%fused_computation.94 | convolution fusion | flops 403716096 | bytes 12582912 | tf_op jit(solution)/shard_map/qb,epbc->eqpc/dot_general | solution.py:26
  351.6 7.8 %fusion.77 = f32[2,16,1024,32]{2,3,1,0:T(8,128)} fusion(f32[2,16,1024,32]{2,3,1,0:T(8,128)S(1)} %fusion.24, f32[2,16,32,1024]{3,1,2,0:T(8,128)S(1)} %get-tuple-element.11), kind=kOutput, calls=%fused_computation.95 | convolution fusion | flops 403716096 | bytes 12582912 | tf_op jit(solution)/shard_map/qb,epbc->eqpc/dot_general | solution.py:26
  359.4 7.7 %fusion.62 = f32[2,16,1024,32]{2,3,1,0:T(8,128)} fusion(f32[2,16,1024,32]{2,3,1,0:T(8,128)S(1)} %fusion.42, f32[2,16,32,1024]{3,1,2,0:T(8,128)S(1)} %get-tuple-element.31), kind=kOutput, calls=%fused_computation.90 | convolution fusion | flops 403716096 | bytes 12582912 | tf_op jit(solution)/shard_map/qb,epbc->eqpc/dot_general | solution.py:26
  367.1 11.2 %multiply_subtract_fusion = (f32[2,16,1024,32]{2,3,1,0:T(8,128)S(1)}, f32[2,16,1024,32]{2,3,1,0:T(8,128)S(1)}) fusion(f32[2,16,1024,32]{2,3,1,0:T(8,128)} %fusion.77, f32[2,16,1024,32]{2,3,1,0:T(8,128)} %fusion.62, f32[2,16,1024,32]{2,3,1,0:T(8,128)S(1)} %copy-done.3, f32[2,16,1024,32]{2,3,1,0:T(8,128)} %fusion.40, ...), kind=kOutput, calls=%fused_computation.40 | convolution fusion | flops 410007552 | bytes 29360128 | tf_op jit(solution)/shard_map/qb,epbc->eqpc/dot_general | solution.py:26
  395.7 6.9 %fusion.2 = (f32[2,32,16,1024]{3,1,2,0:T(8,128)S(1)}, f32[2,32,16,1024]{3,1,2,0:T(8,128)S(1)}) fusion(f32[2,16,1024,32]{2,3,1,0:T(8,128)S(1)} %fusion.84, f32[32,16]{0,1:T(8,128)S(1)} %get-tuple-element.40, f32[32,16]{0,1:T(8,128)S(1)} %get-tuple-element.41, f32[2,16,1024,32]{2,3,1,0:T(8,128)S(1)} %fusion.4, f32[2,16,1024,32]{2,3,1,0:T(8,128)S(1)} %get-tuple-element.5), kind=kOutput, calls=%fused_computation.11 | convolution fusion | flops 410007552 | bytes 20975616 | tf_op jit(solution)/shard_map/bq,eqpc->ebpc/dot_general | solution.py:26
  402.6 8.1 %fusion.18 = f32[2,32,1024,16]{2,3,1,0:T(8,128)S(1)} fusion(f32[2,32,16,1024]{3,1,2,0:T(8,128)S(1)} %get-tuple-element.20), kind=kOutput, calls=%fused_computation.49 | convolution fusion | flops 201330176 | bytes 8388608 | tf_op jit(solution)/shard_map/ap,ebpc->eabc/dot_general | solution.py:26
  410.7 7.8 %fusion.16 = f32[2,32,1024,16]{2,3,1,0:T(8,128)S(1)} fusion(f32[2,32,16,1024]{3,1,2,0:T(8,128)S(1)} %get-tuple-element.20), kind=kOutput, calls=%fused_computation.47 | convolution fusion | flops 201330176 | bytes 8388608 | tf_op jit(solution)/shard_map/ap,ebpc->eabc/dot_general | solution.py:26
  418.6 8.5 %subtract_bitcast_fusion = f32[2,16,32,1024]{3,1,2,0:T(8,128)S(1)} fusion(f32[2,32,1024,16]{2,3,1,0:T(8,128)S(1)} %fusion.18, f32[2,32,16,1024]{3,1,2,0:T(8,128)S(1)} %get-tuple-element.19), kind=kOutput, calls=%fused_computation.38 | convolution fusion | flops 202378752 | bytes 12582912 | tf_op jit(solution)/shard_map/ap,ebpc->eabc/dot_general | solution.py:26
  429.5 8.1 %add_bitcast_fusion = f32[2,16,32,1024]{3,1,2,0:T(8,128)S(1)} fusion(f32[2,32,1024,16]{2,3,1,0:T(8,128)S(1)} %fusion.16, f32[2,32,16,1024]{3,1,2,0:T(8,128)S(1)} %get-tuple-element.19), kind=kOutput, calls=%fused_computation.37 | convolution fusion | flops 202378752 | bytes 12582912 | tf_op jit(solution)/shard_map/ap,ebpc->eabc/dot_general | solution.py:26
  447.9 74.4 %all_to_all.16 = bf16[2,2,1,512,1024]{4,1,2,0,3:T(2,128)(2,1)S(1)} all-to-all(bf16[2,2,1,512,1024]{4,1,2,0,3:T(2,128)(2,1)} %copy.128), channel_id=1, replica_groups=mesh['ctx'=32,'ch'=4] {'ctx'}, dimensions={3} | all-to-all | bytes 8388608 | tf_op jit(solution)/shard_map/all_to_all | solution.py:182
  533.7 21.1 %all_to_all.17 = bf16[32,16,1024]{2,1,0:T(8,128)(2,1)S(1)} all-to-all(bf16[32,16,1024]{2,1,0:T(8,128)(2,1)S(1)} %copy.133), channel_id=1, replica_groups=mesh['ctx'=32,'ch'=4] {'ctx'}, dimensions={0} | all-to-all | bytes 2097152 | tf_op jit(solution)/shard_map/all_to_all | solution.py:188
  563.5 44.5 %reduce-scatter.2.cloned.1.call-done = bf16[512,1024]{1,0:T(8,128)(2,1)} async-done(((bf16[512,4096]{1,0:T(8,128)(2,1)}), bf16[512,1024]{1,0:T(8,128)(2,1)}) %reduce-scatter.2.cloned.1.call-update) | async-done | bytes 1048592 | tf_op jit(solution)/shard_map/reduce_scatter | solution.py:195
  (70 shorter events, 92.4 us)
Async XLA Ops:
  6.5 8.4 %copy-start.4 = (bf16[512,3,1024]{2,0,1:T(8,128)(2,1)S(1)}, bf16[512,3,1024]{2,0,1:T(8,128)(2,1)}, u32[]{:S(2)}) copy-start(bf16[512,3,1024]{2,0,1:T(8,128)(2,1)} %param.5) | copy-start | bytes 9437188
  7.5 7.5 %collective-permute-start = (bf16[2,3,1024]{2,0,1:T(2,128)(2,1)S(1)}, bf16[2,3,1024]{2,0,1:T(2,128)(2,1)S(1)}, u32[]{:S(2)}, u32[]{:S(2)}) collective-permute-start(bf16[2,3,1024]{2,0,1:T(2,128)(2,1)S(1)} %slice.61), channel_id=1, source_target_pairs={{0,4},{4,8},{8,12},{12,16},{16,20},{20,24},{24,28},{28,32},{32,36}... | collective-permute-start | bytes 36872 | tf_op jit(solution)/shard_map/ppermute | solution.py:14
  17.8 2.7 copy-start
  24.0 36.1 %all-to-all-start = ((bf16[2,1,512,1024]{3,0,1,2:T(2,128)(2,1)}), bf16[2,1,512,1024]{3,0,1,2:T(2,128)(2,1)S(1)}, u32[]{:S(2)}, u32[]{:S(2)}) async-start(bf16[2,1,512,1024]{3,0,1,2:T(2,128)(2,1)} %copy.93), calls=%async_computation | async-start | bytes 4194304 | tf_op jit(solution)/shard_map/all_to_all | solution.py:151
  90.3 112.2 %all-to-all-start.1 = ((bf16[2,2,2,32,16,1024]{5,4,2,1,0,3:T(8,128)(2,1)}), bf16[2,2,2,32,16,1024]{5,4,2,1,0,3:T(8,128)(2,1)}, u32[]{:S(2)}, u32[]{:S(2)}) async-start(bf16[2,2,2,32,16,1024]{5,4,2,1,0,3:T(8,128)(2,1)} %copy.104), calls=%async_computation.1 | async-start | bytes 16777216 | tf_op jit(solution)/shard_map/all_to_all | solution.py:170
  95.7 512.3 %reduce-scatter.2.cloned.1.call-start = ((), (), s32[]{:S(2)}) async-start(), calls=%async_computation.5 | async-start | bytes 5242880 | tf_op jit(solution)/shard_map/reduce_scatter | solution.py:195
  310.7 9.2 %copy-start.2 = (f32[2,16,32,1024]{3,1,2,0:T(8,128)S(1)}, f32[2,16,32,1024]{3,1,2,0:T(8,128)}, u32[]{:S(2)}) copy-start(f32[2,16,32,1024]{3,1,2,0:T(8,128)} %get-tuple-element.12) | copy-start | bytes 12582916
  319.9 8.1 %copy-start.1 = (f32[2,16,32,1024]{3,1,2,0:T(8,128)S(1)}, f32[2,16,32,1024]{3,1,2,0:T(8,128)}, u32[]{:S(2)}) copy-start(f32[2,16,32,1024]{3,1,2,0:T(8,128)} %get-tuple-element.30) | copy-start | bytes 12582916
  359.4 7.7 %copy-start.3 = (f32[2,16,1024,32]{2,3,1,0:T(8,128)S(1)}, f32[2,16,1024,32]{2,3,1,0:T(8,128)}, u32[]{:S(2)}) copy-start(f32[2,16,1024,32]{2,3,1,0:T(8,128)} %fusion.74) | copy-start | bytes 12582916
  529.1 26.0 %slice-start = ((s8[6291456]{0:T(1024)(128)(4,1)}), s8[4194304]{0:T(1024)(128)(4,1)S(1)}, s32[]{:S(2)}) async-start(s8[6291456]{0:T(1024)(128)(4,1)} %bitcast.203), calls=%async_computation.6 | async-start | bytes 8388608
  529.7 25.3 %slice-start.1 = ((s8[6291456]{0:T(1024)(128)(4,1)}), s8[2097152]{0:T(1024)(128)(4,1)S(1)}, s32[]{:S(2)}) async-start(s8[6291456]{0:T(1024)(128)(4,1)} %bitcast.203), calls=%async_computation.7 | async-start | bytes 4194304
  533.1 22.0 %copy-start.5 = (f32[1024]{0:T(1024)S(1)}, f32[1024]{0:T(1024)}, u32[]{:S(2)}) copy-start(f32[1024]{0:T(1024)} %param.8) | copy-start | bytes 12292
  533.1 23.1 %slice-start.2 = ((s8[8388608]{0:T(1024)(128)(4,1)}), s8[4194304]{0:T(1024)(128)(4,1)S(1)}, s32[]{:S(2)}) async-start(s8[8388608]{0:T(1024)(128)(4,1)} %bitcast.219), calls=%async_computation.8 | async-start | bytes 8388608
  555.1 2.2 slice-start.3
Sparse Core Ops, SparseCore 0:
  563.6 44.3 reduce-scatter.1
where the time goes:
time: 621 us; the launch traced here: 615 us
  matrix products  216 us (35%)
  waiting for transfers between devices  179 us (29%)
  blocking collectives  95.5 us (15%)
  local copies, waits for them, and re-layouts  60.6 us (10%)
  other arithmetic  31.4 us (5%)
  starting transfers between devices  18.1 us (3%)
  between operations  14.4 us (2%)
    dot_general x30, matrix products, contract(): return jnp.einsum(form, table, values, precision=highest)  210 us
    all_to_all x1, waiting for transfers between devices, on_device(): lax.all_to_all(shortened(stacked), 'ctx', split_axis=3, concat_axis=4, ti...  106 us
    all_to_all x1, blocking collectives, on_device(): lax.all_to_all(shortened(waves), 'ctx', split_axis=3, concat_axis=2, tile...  74.4 us
    reduce_scatter x1, waiting for transfers between devices, on_device(): lax.psum_scatter(terms.astype(jnp.bfloat16), 'ch', scatter_dimension=1, t...  44.5 us
    all_to_all x1, waiting for transfers between devices, on_device(): lax.all_to_all(signals[:, None].astype(jnp.bfloat16), 'ctx', split_axis=2...  28.1 us
    all_to_all x1, blocking collectives, on_device(): lax.all_to_all(shortened(real_rows), 'ctx', split_axis=0, concat_axis=1,...  21.1 us
  transfers between devices with their start and end apart: 4, of which 3 were waited for; matrix products, arithmetic and copies ran while one was open for 1% of the time, Pallas kernels for 0%

commit v1 on v0

v1 whole, which is shorter than its diff:
```python
import functools
import math

import jax
import jax.numpy as jnp
import ml_dtypes
import numpy as np
from jax import lax
from jax.experimental import pallas as pl
from jax.experimental.pallas import tpu as pltpu
from jax.sharding import PartitionSpec as P

GROUP = 16


def tables(blocks, rows):
    classes = 2 * blocks
    half = blocks + 1
    length = classes * rows
    ids, places, blk = np.arange(half), np.arange(rows), np.arange(blocks)
    col = 2.0 * np.pi / classes * (np.outer(ids, blk) % classes)
    eye = np.eye(GROUP)
    first = np.concatenate([np.cos(col), -np.sin(col)[1:blocks]])
    weight = np.full((half, 1), 2.0)
    weight[0] = weight[blocks] = 1.0
    last = np.concatenate([weight * np.cos(col), (-weight * np.sin(col))[1:blocks]]).T / length
    twist = 2.0 * np.pi / length * (np.outer(ids, places) % length)
    inner = 2.0 * np.pi / rows * (np.outer(places, places) % rows)
    cos, sin = np.cos(inner), np.sin(inner)
    square = np.block([[cos, -sin], [sin, cos]])
    return (
        np.kron(first, eye).astype(ml_dtypes.bfloat16),
        np.kron(last, eye).astype(ml_dtypes.bfloat16),
        square.astype(ml_dtypes.bfloat16),
        np.cos(twist).astype(np.float32)[:, None, :],
        np.sin(twist).astype(np.float32)[:, None, :],
    )


def mul(left, right):
    return jnp.dot(left, right, preferred_element_type=jnp.float32)


def conv_kernel(blocks, rows, d_ref, h_ref, first, last, square, tw_cos, tw_sin, out_ref, col, turned, spec_d, spec_h, wide):
    half = blocks + 1
    chans = d_ref.shape[1]

    def forward(src, g, spec):
        x = src[:, pl.ds(g * GROUP, GROUP), :].reshape(blocks * GROUP, rows)
        col[...] = mul(first[...], x).reshape(2 * blocks, GROUP, rows)
        for k in range(half):
            c, s = tw_cos[k], tw_sin[k]
            re = col[k]
            if 0 < k < blocks:
                im = col[blocks + k]
                a, b = re * c + im * s, im * c - re * s
            else:
                a, b = re * c, -(re * s)
            turned[k, :, :rows] = a.astype(jnp.bfloat16)
            turned[k, :, rows:] = b.astype(jnp.bfloat16)
        spec[...] = mul(turned[...].reshape(half * GROUP, 2 * rows), square[...])

    def group(g, carry):
        forward(h_ref, g, spec_h)
        forward(d_ref, g, spec_d)
        a, b = spec_d[:, :rows], spec_d[:, rows:]
        u, v = spec_h[:, :rows], spec_h[:, rows:]
        flat = turned.reshape(half * GROUP, 2 * rows)
        flat[:, :rows] = (a * v + b * u).astype(jnp.bfloat16)
        flat[:, rows:] = (a * u - b * v).astype(jnp.bfloat16)
        spec_d[...] = mul(flat[...], square[...])
        back = spec_d.reshape(half, GROUP, 2 * rows)
        for k in range(half):
            c, s = tw_cos[k], tw_sin[k]
            im, re = back[k, :, :rows], back[k, :, rows:]
            wide[k] = (re * c - im * s).astype(jnp.bfloat16)
            if 0 < k < blocks:
                wide[blocks + k] = (im * c + re * s).astype(jnp.bfloat16)
        y = mul(last[...], wide[...].reshape(2 * blocks * GROUP, rows))
        out_ref[:, pl.ds(g * GROUP, GROUP), :] = y.reshape(blocks, GROUP, rows).astype(out_ref.dtype)
        return carry

    lax.fori_loop(0, chans // GROUP, group, 0)


def long_convolution(d, h):
    blocks, chans, rows = d.shape
    half = blocks + 1
    return pl.pallas_call(
        functools.partial(conv_kernel, blocks, rows),
        out_shape=jax.ShapeDtypeStruct(d.shape, jnp.bfloat16),
        in_specs=[pl.BlockSpec(memory_space=pltpu.VMEM)] * 7,
        out_specs=pl.BlockSpec(memory_space=pltpu.VMEM),
        scratch_shapes=[
            pltpu.VMEM((2 * blocks, GROUP, rows), jnp.float32),
            pltpu.VMEM((half, GROUP, 2 * rows), jnp.bfloat16),
            pltpu.VMEM((half * GROUP, 2 * rows), jnp.float32),
            pltpu.VMEM((half * GROUP, 2 * rows), jnp.float32),
            pltpu.VMEM((2 * blocks, GROUP, rows), jnp.bfloat16),
        ],
        compiler_params=pltpu.CompilerParams(vmem_limit_bytes=48 * 2**20),
        name="long_convolution",
    )(d, h, *tables(blocks, rows))


def passed_along(array, axis, by):
    count = lax.axis_size(axis)
    pairs = [(i, i + by) for i in range(count) if 0 <= i + by < count]
    return lax.ppermute(array, axis, pairs)


def on_device(branches, short_kernel, long_filter, skip_gain, out_weight):
    count = lax.axis_size("ctx")
    rows, _, chans = branches.shape
    taps = short_kernel.shape[0]

    def to_channels(x):
        x = x.astype(jnp.bfloat16).T.reshape(count, chans // count, rows)
        return lax.all_to_all(x, "ctx", split_axis=0, concat_axis=0, tiled=True)

    h = to_channels(long_filter)
    earlier = passed_along(branches[rows - (taps - 1):], "ctx", 1)
    extended = jnp.concatenate([earlier, branches], axis=0).astype(jnp.float32)
    featured = sum(
        short_kernel[j][None] * extended[taps - 1 - j:taps - 1 - j + rows] for j in range(taps)
    )
    query = featured[:, 0]
    driven = featured[:, 1] * featured[:, 2]
    d = to_channels(driven)
    y = long_convolution(d, h)
    y = lax.all_to_all(y, "ctx", split_axis=0, concat_axis=0, tiled=True)
    conv = y.reshape(chans, rows).T.astype(jnp.float32)
    gated = (query * (conv + skip_gain * driven)).astype(jnp.bfloat16)
    terms = jnp.dot(gated, out_weight, preferred_element_type=jnp.float32)
    return lax.psum_scatter(terms.astype(jnp.bfloat16), "ch", scatter_dimension=1, tiled=True)


def solution(mesh):
    placed = (P("ctx", None, "ch"), P(None, None, "ch"), P("ctx", "ch"), P("ch"), P("ch", None))
    return jax.shard_map(
        on_device, mesh=mesh, in_specs=placed, out_specs=P("ctx", "ch"), check_vma=False
    )
```

time: 621 us -> 161 us (0.26)
  matrix products: 216 us -> 12.5 us
  waiting for transfers between devices: 179 us -> 50.4 us
  blocking collectives: 95.5 us -> 41.5 us
  local copies, waits for them, and re-layouts: 60.6 us -> 9.01 us
  other arithmetic: 31.4 us -> 8.07 us
  Pallas kernels: 0 us -> 12.7 us
    dot_general x30 -> x0, matrix products: 210 us -> none  [contract(): return jnp.einsum(form, table, values, precision=highest)]
    all_to_all x2 -> x1, waiting for transfers between devices: 134 us -> 5.83 us  [to_channels(): return lax.all_to_all(x, 'ctx', split_axis=0, concat_axis=0, tiled=True)]
    all_to_all x2, blocking collectives: 95.5 us -> 41.5 us  [the longest x1 20.9 us: to_channels(): return lax.all_to_all(x, 'ctx', split_axis=0, concat_axis=0, tiled=True)]
    another operation x3 -> x0, local copies, waits for them, and re-layouts: 21.1 us -> none  [the longest x1 11.3 us: on_device(): stacked = jnp.stack([jnp.stack(driven_cols), jnp.stack(filter_cols)])]
    slice x4 -> x1, local copies, waits for them, and re-layouts: 19.4 us -> 0.82 us  [on_device(): earlier = passed_along(branches[rows - (taps - 1):], 'ctx', 1)]
    pallas_call x0 -> x1, Pallas kernels: none -> 12.7 us  [long_convolution(): pl.pallas_call(functools.partial(conv_kernel, blocks, rows), out_shape=ja...]
    convert_element_type x2 -> x1, other arithmetic: 12.3 us -> 0.35 us  [on_device(): conv = y.reshape(chans, rows).T.astype(jnp.float32)]
    all_to_all x1 -> x0, local copies, waits for them, and re-layouts: 8.56 us -> none  [on_device(): lax.all_to_all(shortened(stacked), 'ctx', split_axis=3, concat_axis=4, ti...]
  transfers between devices with their start and end apart: 4 -> 3, of which waited for: 3 -> 2; matrix products, arithmetic and copies ran while one was open for 1% -> 7% of each run, Pallas kernels for 0% -> 0%
where the time goes in v1:
time: 161 us; the launch traced here: 160 us
  waiting for transfers between devices  50.4 us (31%)
  blocking collectives  41.5 us (26%)
  between operations  13.5 us (8%)
  starting transfers between devices  12.7 us (8%)
  Pallas kernels  12.7 us (8%)
  matrix products  12.5 us (8%)
  local copies, waits for them, and re-layouts  9.01 us (6%)
  other arithmetic  8.07 us (5%)
    reduce_scatter x1, waiting for transfers between devices, on_device(): lax.psum_scatter(terms.astype(jnp.bfloat16), 'ch', scatter_dimension=1, t...  44.6 us
    all_to_all x1, blocking collectives, to_channels(): return lax.all_to_all(x, 'ctx', split_axis=0, concat_axis=0, tiled=True)  20.9 us
    all_to_all x1, blocking collectives, on_device(): y = lax.all_to_all(y, 'ctx', split_axis=0, concat_axis=0, tiled=True)  20.7 us
    pallas_call x1, Pallas kernels, long_convolution(): pl.pallas_call(functools.partial(conv_kernel, blocks, rows), out_shape=ja...  12.7 us
    dot_general x1, matrix products, on_device(): terms = jnp.dot(gated, out_weight, preferred_element_type=jnp.float32)  12.5 us
    all_to_all x1, starting transfers between devices, to_channels(): return lax.all_to_all(x, 'ctx', split_axis=0, concat_axis=0, tiled=True)  7.76 us
    all_to_all x1, waiting for transfers between devices, to_channels(): return lax.all_to_all(x, 'ctx', split_axis=0, concat_axis=0, tiled=True)  5.83 us
    ppermute x1, starting transfers between devices, passed_along(): return lax.ppermute(array, axis, pairs)  4.94 us
  transfers between devices with their start and end apart: 3, of which 2 were waited for; matrix products, arithmetic and copies ran while one was open for 7% of the time, Pallas kernels for 0%

profile of v1, /device:TPU:1, one launch (start us, length us, event | category | flops | bytes accessed | tf_op | source)
XLA Modules:
  0.0 160.4 jit_solution(6930835379008055645)
XLA Ops:
  6.5 0.0 copy-start.5
  6.5 0.8 slice.31
  7.4 4.9 %collective-permute-start = (bf16[2,3,1024]{2,0,1:T(2,128)(2,1)S(1)}, bf16[2,3,1024]{2,0,1:T(2,128)(2,1)S(1)}, u32[]{:S(2)}, u32[]{:S(2)}) collective-permute-start(bf16[2,3,1024]{2,0,1:T(2,128)(2,1)S(1)} %slice.31), channel_id=1, source_target_pairs={{0,4},{4,8},{8,12},{12,16},{16,20},{20,24},{24,28},{28,32},{32,36}... | collective-permute-start | bytes 36872 | tf_op jit(solution)/shard_map/ppermute | solution.py:109
  12.3 1.8 %convert_bitcast_fusion = bf16[1024,512]{0,1:T(8,128)(2,1)S(1)} fusion(f32[512,1024]{1,0:T(8,128)} %param.12), kind=kLoop, calls=%fused_computation.15 | loop fusion | flops 524288 | bytes 3145728 | tf_op jit(solution)/shard_map/transpose | solution.py:118
  14.1 1.3 copy.12
  15.4 7.8 %all-to-all-start.1 = ((bf16[32,32,512]{2,1,0:T(8,128)(2,1)}), bf16[32,32,512]{2,1,0:T(8,128)(2,1)S(1)}, u32[]{:S(2)}, u32[]{:S(2)}) async-start(bf16[32,32,512]{2,1,0:T(8,128)(2,1)} %bitcast.8), calls=%async_computation.1 | async-start | bytes 2097152 | tf_op jit(solution)/shard_map/all_to_all | solution.py:119
  23.2 0.0 reduce-scatter.2.cloned.1.call-start
  23.2 0.0 copy-done.5
  23.2 0.0 collective-permute-done
  23.2 2.8 %maximum_convert_fusion = f32[514,3,1024]{2,0,1:T(8,128)S(1)} fusion(bf16[512,3,1024]{2,0,1:T(8,128)(2,1)} %param.10, bf16[2,3,1024]{2,0,1:T(2,128)(2,1)S(1)} %collective-permute-done), kind=kLoop, calls=%fused_computation.6 | loop fusion | flops 6316032 | bytes 9474048 | tf_op jit(solution)/shard_map/convert_element_type | solution.py:123
  26.1 1.9 %fusion = f32[512,3,1024]{2,0,1:T(8,128)S(1)} fusion(f32[514,3,1024]{2,0,1:T(8,128)S(1)} %maximum_convert_fusion, f32[3,1024]{1,0:T(4,128)S(1)} %get-tuple-element.6, f32[3,1024]{1,0:T(4,128)S(1)} %get-tuple-element.7, f32[3,1024]{1,0:T(4,128)S(1)} %get-tuple-element.5), kind=kLoop, calls=%fused_computation.1 | loop fusion | flops 7864320 | bytes 25202688 | tf_op jit(solution)/shard_map/add | solution.py:124
  27.9 0.0 copy-start.4
  28.0 2.6 %copy-done.4 = f32[512,3,1024]{2,0,1:T(8,128)} copy-done((f32[512,3,1024]{2,0,1:T(8,128)}, f32[512,3,1024]{2,0,1:T(8,128)S(1)}, u32[]{:S(2)}) %copy-start.4) | copy-done | bytes 6291480
  30.6 0.0 copy-start
  30.6 0.0 copy-start.1
  30.6 1.3 convert_bitcast_fusion.1
  31.9 2.3 %copy.11 = bf16[1024,512]{1,0:T(8,128)(2,1)} copy(bf16[1024,512]{0,1:T(8,128)(2,1)} %convert_bitcast_fusion.1) | data formatting | bytes 2097152 | tf_op jit(solution)/shard_map/transpose | solution.py:118
  34.2 5.8 %all-to-all-done.1.h_ref = bf16[32,32,512]{2,1,0:T(8,128)(2,1)S(1)} async-done(((bf16[32,32,512]{2,1,0:T(8,128)(2,1)}), bf16[32,32,512]{2,1,0:T(8,128)(2,1)S(1)}, u32[]{:S(2)}, u32[]{:S(2)}) %all-to-all-start.1) | async-done | bytes 1048608 | tf_op jit(solution)/shard_map/all_to_all | solution.py:119
  40.1 20.9 %all_to_all.15.d_ref = bf16[32,32,512]{2,1,0:T(8,128)(2,1)S(1)} all-to-all(bf16[32,32,512]{2,1,0:T(8,128)(2,1)} %bitcast.35), channel_id=1, replica_groups=mesh['ctx'=32,'ch'=4] {'ctx'}, dimensions={0} | all-to-all | bytes 2097152 | tf_op jit(solution)/shard_map/all_to_all | solution.py:119
  60.9 0.0 copy-done
  60.9 0.0 copy-done.1
  60.9 0.0 copy-done.2
  60.9 0.0 copy-done.3
  61.0 12.7 %long_convolution.1 = bf16[32,32,512]{2,1,0:T(8,128)(2,1)S(1)} custom-call(bf16[32,32,512]{2,1,0:T(8,128)(2,1)S(1)} %all_to_all.15.d_ref, bf16[32,32,512]{2,1,0:T(8,128)(2,1)S(1)} %all-to-all-done.1.h_ref, bf16[1024,512]{1,0:T(8,128)(2,1)S(1)} %copy-done, bf16[512,1024]{1,0:T(8,128)(2,1)S(1)} %copy-done.1, bf16[1024,1024]{1,0:T(8,128)(2,1)} %constant.12.clone.square, ...), custom_call_target="tpu_custom_call" | custom-call | tf_op jit(solution)/shard_map/long_convolution/pallas_call | solution.py:89
  73.6 0.0 copy-start.6
  73.6 20.7 %all_to_all.16 = bf16[32,32,512]{2,1,0:T(8,128)(2,1)S(1)} all-to-all(bf16[32,32,512]{2,1,0:T(8,128)(2,1)S(1)} %long_convolution.1), channel_id=1, replica_groups=mesh['ctx'=32,'ch'=4] {'ctx'}, dimensions={0} | all-to-all | bytes 2097152 | tf_op jit(solution)/shard_map/all_to_all | solution.py:131
  94.3 0.3 bitcast_convert_fusion
  94.7 1.8 %copy.13 = f32[1024,512]{0,1:T(8,128)} copy(f32[1024,512]{1,0:T(8,128)S(1)} %bitcast_convert_fusion) | data formatting | bytes 4194304 | tf_op jit(solution)/shard_map/convert_element_type | solution.py:132
  96.5 0.0 copy-done.6
  96.5 12.5 %convolution_convert_fusion = bf16[512,4096]{1,0:T(8,128)(2,1)} fusion(bf16[1024,4096]{1,0:T(8,128)(2,1)} %param.14, f32[512,3,1024]{2,0,1:T(8,128)} %copy-done.4, f32[1024,512]{0,1:T(8,128)} %copy.13, f32[1024]{0:T(1024)S(1)} %copy-done.6), kind=kOutput, calls=%fused_computation.5 | convolution fusion | flops 4299685888 | bytes 20975616 | tf_op jit(solution)/shard_map/dot_general | solution.py:134
  109.0 0.0 reduce-scatter.2.cloned.1.call-update
  109.0 44.6 %reduce-scatter.2.cloned.1.call-done = bf16[512,1024]{1,0:T(8,128)(2,1)} async-done(((bf16[512,4096]{1,0:T(8,128)(2,1)}), bf16[512,1024]{1,0:T(8,128)(2,1)}) %reduce-scatter.2.cloned.1.call-update) | async-done | bytes 1048592 | tf_op jit(solution)/shard_map/reduce_scatter | solution.py:135
  (3 shorter events, 0.0 us)
Async XLA Ops:
  6.5 16.7 %copy-start.5 = (f32[3,3,1024]{2,1,0:T(4,128)S(1)}, f32[3,3,1024]{2,1,0:T(4,128)}, u32[]{:S(2)}) copy-start(f32[3,3,1024]{2,1,0:T(4,128)} %param.11) | copy-start | bytes 110596
  7.4 15.9 %collective-permute-start = (bf16[2,3,1024]{2,0,1:T(2,128)(2,1)S(1)}, bf16[2,3,1024]{2,0,1:T(2,128)(2,1)S(1)}, u32[]{:S(2)}, u32[]{:S(2)}) collective-permute-start(bf16[2,3,1024]{2,0,1:T(2,128)(2,1)S(1)} %slice.31), channel_id=1, source_target_pairs={{0,4},{4,8},{8,12},{12,16},{16,20},{20,24},{24,28},{28,32},{32,36}... | collective-permute-start | bytes 36872 | tf_op jit(solution)/shard_map/ppermute | solution.py:109
  15.4 24.7 %all-to-all-start.1 = ((bf16[32,32,512]{2,1,0:T(8,128)(2,1)}), bf16[32,32,512]{2,1,0:T(8,128)(2,1)S(1)}, u32[]{:S(2)}, u32[]{:S(2)}) async-start(bf16[32,32,512]{2,1,0:T(8,128)(2,1)} %bitcast.8), calls=%async_computation.1 | async-start | bytes 2097152 | tf_op jit(solution)/shard_map/all_to_all | solution.py:119
  23.2 130.4 %reduce-scatter.2.cloned.1.call-start = ((), (), s32[]{:S(2)}) async-start(), calls=%async_computation.4 | async-start | bytes 5242880 | tf_op jit(solution)/shard_map/reduce_scatter | solution.py:135
  27.9 2.7 %copy-start.4 = (f32[512,3,1024]{2,0,1:T(8,128)}, f32[512,3,1024]{2,0,1:T(8,128)S(1)}, u32[]{:S(2)}) copy-start(f32[512,3,1024]{2,0,1:T(8,128)S(1)} %fusion) | copy-start | bytes 18874372
  30.6 30.3 %copy-start = (bf16[1024,512]{1,0:T(8,128)(2,1)S(1)}, bf16[1024,512]{1,0:T(8,128)(2,1)}, u32[]{:S(2)}) copy-start(bf16[1024,512]{1,0:T(8,128)(2,1)} %constant.10.clone.first) | copy-start | bytes 3145732
  30.6 30.3 %copy-start.1 = (bf16[512,1024]{1,0:T(8,128)(2,1)S(1)}, bf16[512,1024]{1,0:T(8,128)(2,1)}, u32[]{:S(2)}) copy-start(bf16[512,1024]{1,0:T(8,128)(2,1)} %constant.11.clone.last) | copy-start | bytes 3145732
  30.6 30.3 %copy-start.2 = (f32[33,1,512]{2,1,0:T(1,128)S(1)}, f32[33,1,512]{2,1,0:T(1,128)}, u32[]{:S(2)}) copy-start(f32[33,1,512]{2,1,0:T(1,128)} %constant.13.clone.tw_cos) | copy-start | bytes 202756
  30.6 30.3 %copy-start.3 = (f32[33,1,512]{2,1,0:T(1,128)S(1)}, f32[33,1,512]{2,1,0:T(1,128)}, u32[]{:S(2)}) copy-start(f32[33,1,512]{2,1,0:T(1,128)} %constant.14.clone.tw_sin) | copy-start | bytes 202756
  73.6 22.9 %copy-start.6 = (f32[1024]{0:T(1024)S(1)}, f32[1024]{0:T(1024)}, u32[]{:S(2)}) copy-start(f32[1024]{0:T(1024)} %param.13) | copy-start | bytes 12292
Sparse Core Ops, SparseCore 0:
  109.1 44.3 reduce-scatter.1

commit v2 on v1

v2 whole, which is shorter than its diff:
```python
import functools

import jax
import jax.numpy as jnp
import ml_dtypes
import numpy as np
from jax import lax
from jax.experimental import pallas as pl
from jax.experimental.pallas import tpu as pltpu
from jax.sharding import PartitionSpec as P

MESH = pl.DeviceIdType.MESH
GROUP = 16
TILE = 128


def tables(blocks, rows):
    classes = 2 * blocks
    half = blocks + 1
    length = classes * rows
    ids, places, blk = np.arange(half), np.arange(rows), np.arange(blocks)
    col = 2.0 * np.pi / classes * (np.outer(ids, blk) % classes)
    eye = np.eye(GROUP)
    first = np.concatenate([np.cos(col), -np.sin(col)[1:blocks]])
    weight = np.full((half, 1), 2.0)
    weight[0] = weight[blocks] = 1.0
    last = np.concatenate([weight * np.cos(col), (-weight * np.sin(col))[1:blocks]]).T / length
    twist = 2.0 * np.pi / length * (np.outer(ids, places) % length)
    inner = 2.0 * np.pi / rows * (np.outer(places, places) % rows)
    cos, sin = np.cos(inner), np.sin(inner)
    square = np.block([[cos, -sin], [sin, cos]])
    return (
        np.kron(first, eye).astype(ml_dtypes.bfloat16),
        np.kron(last, eye).astype(ml_dtypes.bfloat16),
        square.astype(ml_dtypes.bfloat16),
        np.cos(twist).astype(np.float32)[:, None, :],
        np.sin(twist).astype(np.float32)[:, None, :],
    )


def mul(left, right):
    return jnp.dot(left, right, preferred_element_type=jnp.float32)


def loop(count, body, start=0):
    def step(i, carry):
        body(i)
        return carry

    lax.fori_loop(start, count, step, 0)


def kernel(
    blocks, ring,
    br_in, taps_ref, filt_in, skip_ref, w_in, first_in, last_in, square_in, cos_in, sin_in,
    out_ref,
    br, filt, w, first, last, square, tw_cos, tw_sin,
    halo, h_send, d_send, h_recv, d_recv, y_send, y_recv,
    query, direct, gated, own,
    col, turned, spec_d, spec_h, wide,
    s1, r1, s2, r2,
    in_sem, halo_sem, h_sem, d_sem, y_sem, r1_sem, r2_sem, send_sem,
):
    me = lax.axis_index("ctx")
    x = lax.axis_index("ch")
    _, rows, chans = br.shape
    share = chans // blocks
    groups = share // GROUP
    half = blocks + 1
    quarters = rows // TILE
    right, left = lax.rem(x + 1, ring), lax.rem(x + ring - 1, ring)

    inputs = [
        pltpu.make_async_copy(src, dst, in_sem.at[i])
        for i, (src, dst) in enumerate([
            (filt_in, filt), (br_in, br), (first_in, first), (cos_in, tw_cos), (sin_in, tw_sin),
            (square_in, square), (last_in, last), (w_in, w),
        ])
    ]
    for copy in inputs:
        copy.start()

    barrier = pltpu.get_barrier_semaphore()

    def greet(k):
        pl.semaphore_signal(
            barrier, inc=1, device_id={"ctx": lax.rem(me + k, blocks)}, device_id_type=MESH
        )

    loop(blocks, greet, 1)
    for side in (left, right):
        pl.semaphore_signal(barrier, inc=1, device_id={"ch": side}, device_id_type=MESH)

    def lanes(i):
        return pl.ds(pl.multiple_of(i * TILE, TILE), TILE)

    def turn_filter(i):
        for r in range(quarters):
            here = slice(r * TILE, (r + 1) * TILE)
            h_send[lanes(i), here] = filt[here, lanes(i)].T.astype(jnp.bfloat16)

    def feature(r, i):
        here = slice(r * TILE, (r + 1) * TILE)
        feats = []
        for b in range(3):
            if r:
                part = br[b, r * TILE - GROUP:(r + 1) * TILE, lanes(i)].astype(jnp.float32)
            else:
                before = halo[b, :, lanes(i)].astype(jnp.float32)
                before = jnp.where(me > 0, before, jnp.zeros_like(before))
                part = jnp.concatenate([before, br[b, here, lanes(i)].astype(jnp.float32)], axis=0)
            total = taps_ref[0, b:b + 1, lanes(i)] * part[GROUP:]
            for j in (1, 2):
                total = total + taps_ref[j, b:b + 1, lanes(i)] * pltpu.roll(part, j, 0)[GROUP:]
            feats.append(total)
        driven = feats[1] * feats[2]
        query[here, lanes(i)] = feats[0]
        direct[here, lanes(i)] = skip_ref[:, lanes(i)] * driven
        d_send[lanes(i), here] = driven.T.astype(jnp.bfloat16)

    inputs[0].wait()
    loop(chans // TILE, turn_filter)
    inputs[1].wait()
    for r in range(1, quarters):
        loop(chans // TILE, functools.partial(feature, r))

    pl.semaphore_wait(barrier, blocks - 1 + 2)

    halo_copy = pltpu.make_async_remote_copy(
        src_ref=br.at[:, pl.ds(rows - GROUP, GROUP), :],
        dst_ref=halo,
        send_sem=send_sem.at[0],
        recv_sem=halo_sem.at[0],
        device_id={"ctx": lax.rem(me + 1, blocks)},
        device_id_type=MESH,
    )
    halo_copy.start()

    def scatter(src, dst, send, recv):
        def one(k):
            t = lax.rem(me + k, blocks)
            pltpu.make_async_remote_copy(
                src_ref=src(t), dst_ref=dst, send_sem=send, recv_sem=recv,
                device_id={"ctx": t}, device_id_type=MESH,
            ).start()

        loop(blocks, one, 1)
        pltpu.make_async_copy(src(me), dst, recv).start()

    def block(t):
        return pl.ds(pl.multiple_of(t * share, share), share)

    def part_of(t, g):
        return pl.ds(pl.multiple_of(t * share + g * GROUP, GROUP), GROUP)

    scatter(lambda t: h_send.at[block(t)], h_recv.at[me], send_sem.at[1], h_sem.at[0])
    halo_copy.wait_recv()
    loop(chans // TILE, functools.partial(feature, 0))
    for g in range(groups):
        scatter(lambda t: d_send.at[part_of(t, g)], d_recv.at[g, me], send_sem.at[2], d_sem.at[g])

    def arrived(ref, sem):
        pltpu.make_async_copy(ref, ref, sem).wait()

    def forward(blocks_in, spec):
        col[...] = mul(first[...], blocks_in.reshape(blocks * GROUP, rows)).reshape(2 * blocks, GROUP, rows)
        for k in range(half):
            c, s = tw_cos[k], tw_sin[k]
            re = col[k]
            if 0 < k < blocks:
                im = col[blocks + k]
                a, b = re * c + im * s, im * c - re * s
            else:
                a, b = re * c, -(re * s)
            turned[k, :, :rows] = a.astype(jnp.bfloat16)
            turned[k, :, rows:] = b.astype(jnp.bfloat16)
        spec[...] = mul(turned[...].reshape(half * GROUP, 2 * rows), square[...])

    for copy in inputs[2:7]:
        copy.wait()
    arrived(h_recv, h_sem.at[0])

    def filter_group(g):
        forward(h_recv[:, pl.ds(pl.multiple_of(g * GROUP, GROUP), GROUP), :], spec_h.at[g])

    loop(groups, filter_group)

    def driven_group(g):
        arrived(d_recv.at[g], d_sem.at[g])
        forward(d_recv[g], spec_d)
        a, b = spec_d[:, :rows], spec_d[:, rows:]
        u, v = spec_h[g, :, :rows], spec_h[g, :, rows:]
        flat = turned.reshape(half * GROUP, 2 * rows)
        flat[:, :rows] = (a * v + b * u).astype(jnp.bfloat16)
        flat[:, rows:] = (a * u - b * v).astype(jnp.bfloat16)
        spec_d[...] = mul(flat[...], square[...])
        back = spec_d.reshape(half, GROUP, 2 * rows)
        for k in range(half):
            c, s = tw_cos[k], tw_sin[k]
            im, re = back[k, :, :rows], back[k, :, rows:]
            wide[k] = (re * c - im * s).astype(jnp.bfloat16)
            if 0 < k < blocks:
                wide[blocks + k] = (im * c + re * s).astype(jnp.bfloat16)
        y = mul(last[...], wide[...].reshape(2 * blocks * GROUP, rows)).astype(jnp.bfloat16)
        for q in range(quarters):
            y_send[q, :, pl.ds(pl.multiple_of(g * GROUP, GROUP), GROUP), :] = y[
                :, q * TILE:(q + 1) * TILE
            ].reshape(blocks, GROUP, TILE)

    loop(groups, driven_group)

    def give_back(q):
        scatter(lambda t: y_send.at[q, t], y_recv.at[q, me], send_sem.at[3], y_sem.at[q])

    loop(quarters, give_back)
    inputs[7].wait()

    def quarter(q):
        return pl.ds(pl.multiple_of(q * TILE, TILE), TILE)

    def project(q, target):
        columns = pl.ds(pl.multiple_of(target * chans, chans), chans)
        return mul(gated[quarter(q)], w[:, columns])

    def push(src, dst, send, recv, side):
        pltpu.make_async_remote_copy(
            src_ref=src, dst_ref=dst, send_sem=send, recv_sem=recv,
            device_id={"ch": side}, device_id_type=MESH,
        ).start()

    def opposite(q):
        arrived(y_recv.at[q], y_sem.at[q])

        def gate(i):
            per = TILE // share
            turned_back = y_recv[q, pl.ds(i * per, per)].reshape(TILE, TILE).astype(jnp.float32).T
            value = query[quarter(q), lanes(i)] * (turned_back + direct[quarter(q), lanes(i)])
            gated[quarter(q), lanes(i)] = value.astype(jnp.bfloat16)

        loop(chans // TILE, gate)
        terms = project(q, lax.rem(x + 2, ring)).astype(jnp.bfloat16)
        s1[0, q] = terms[:TILE // 2]
        s1[1, q] = terms[TILE // 2:]
        push(s1.at[0, q], r1.at[0, q], send_sem.at[4], r1_sem.at[0, q], right)
        push(s1.at[1, q], r1.at[1, q], send_sem.at[4], r1_sem.at[1, q], left)

    def beside(q):
        for side, (target, lo, hi) in enumerate([(right, 0, TILE // 2), (left, TILE // 2, TILE)]):
            terms = project(q, target)
            arrived(r1.at[side, q], r1_sem.at[side, q])
            s2[side, q, lo:hi] = (terms[lo:hi] + r1[side, q].astype(jnp.float32)).astype(jnp.bfloat16)
            other = slice(TILE // 2 - lo, TILE + TILE // 2 - hi)
            s2[side, q, other] = terms[other].astype(jnp.bfloat16)
            push(s2.at[side, q], r2.at[side, q], send_sem.at[5], r2_sem.at[side, q], target)
        own[quarter(q)] = project(q, x)

    opposite(0)

    def steady(q):
        opposite(q + 1)
        beside(q)

    loop(quarters - 1, steady)
    beside(quarters - 1)

    def finish(q):
        for side in range(2):
            arrived(r2.at[side, q], r2_sem.at[side, q])
        total = own[quarter(q)] + r2[0, q].astype(jnp.float32) + r2[1, q].astype(jnp.float32)
        out_ref[quarter(q)] = total.astype(out_ref.dtype)

    loop(quarters, finish)

    halo_copy.wait_send()
    arrived(h_send.at[pl.ds(0, chans - share)], send_sem.at[1])
    arrived(d_send.at[pl.ds(0, chans - share)], send_sem.at[2])
    others = y_send.at[:, pl.ds(0, blocks - 1)]
    arrived(others, send_sem.at[3])
    arrived(s1, send_sem.at[4])
    arrived(s2, send_sem.at[5])


def on_device(branches, short_kernel, long_filter, skip_gain, out_weight):
    blocks, ring = lax.axis_size("ctx"), lax.axis_size("ch")
    rows, _, chans = branches.shape
    share, half, quarters = chans // blocks, blocks + 1, rows // TILE
    groups = share // GROUP
    bf16, f32 = jnp.bfloat16, jnp.float32
    consts = tables(blocks, rows)
    anywhere, vmem = pl.BlockSpec(memory_space=pl.ANY), pl.BlockSpec(memory_space=pltpu.VMEM)
    dma = pltpu.SemaphoreType.DMA
    scratch = [
        pltpu.VMEM((3, rows, chans), bf16),
        pltpu.VMEM((rows, chans), f32),
        pltpu.VMEM(out_weight.shape, bf16),
        *[pltpu.VMEM(t.shape, t.dtype) for t in consts],
        pltpu.VMEM((3, GROUP, chans), bf16),
        pltpu.VMEM((chans, rows), bf16),
        pltpu.VMEM((chans, rows), bf16),
        pltpu.VMEM((blocks, share, rows), bf16),
        pltpu.VMEM((groups, blocks, GROUP, rows), bf16),
        pltpu.VMEM((quarters, blocks, share, TILE), bf16),
        pltpu.VMEM((quarters, blocks, share, TILE), bf16),
        pltpu.VMEM((rows, chans), f32),
        pltpu.VMEM((rows, chans), f32),
        pltpu.VMEM((rows, chans), bf16),
        pltpu.VMEM((rows, chans), f32),
        pltpu.VMEM((2 * blocks, GROUP, rows), f32),
        pltpu.VMEM((half, GROUP, 2 * rows), bf16),
        pltpu.VMEM((half * GROUP, 2 * rows), f32),
        pltpu.VMEM((groups, half * GROUP, 2 * rows), f32),
        pltpu.VMEM((2 * blocks, GROUP, rows), bf16),
        pltpu.VMEM((2, quarters, TILE // 2, chans), bf16),
        pltpu.VMEM((2, quarters, TILE // 2, chans), bf16),
        pltpu.VMEM((2, quarters, TILE, chans), bf16),
        pltpu.VMEM((2, quarters, TILE, chans), bf16),
        dma((8,)), dma((1,)), dma((1,)), dma((groups,)), dma((quarters,)),
        dma((2, quarters)), dma((2, quarters)), dma((6,)),
    ]
    return pl.pallas_call(
        functools.partial(kernel, blocks, ring),
        out_shape=jax.ShapeDtypeStruct((rows, chans), bf16),
        in_specs=[anywhere, vmem, anywhere, vmem] + [anywhere] * 6,
        out_specs=vmem,
        scratch_shapes=scratch,
        compiler_params=pltpu.CompilerParams(
            collective_id=0, has_side_effects=True, vmem_limit_bytes=60 * 2**20
        ),
        name="hyena_operator",
    )(
        jnp.transpose(branches, (1, 0, 2)), short_kernel, long_filter, skip_gain.reshape(1, chans),
        out_weight, *consts,
    )


def solution(mesh):
    placed = (P("ctx", None, "ch"), P(None, None, "ch"), P("ctx", "ch"), P("ch"), P("ch", None))
    return jax.shard_map(
        on_device, mesh=mesh, in_specs=placed, out_specs=P("ctx", "ch"), check_vma=False
    )
```

time: 161 us -> 96 us (0.60)
  Pallas kernels: 12.7 us -> 93.5 us
  waiting for transfers between devices: 50.4 us -> 0 us
  blocking collectives: 41.5 us -> 0 us
  between operations: 13.5 us -> 0.01 us
  starting transfers between devices: 12.7 us -> 0 us
  matrix products: 12.5 us -> 0 us
  other arithmetic: 8.07 us -> 0 us
  local copies, waits for them, and re-layouts: 9.01 us -> 2.26 us
    pallas_call x1, Pallas kernels: 12.7 us -> 93.5 us  [on_device(): pl.pallas_call(functools.partial(kernel, blocks, ring), out_shape=jax.Sha...]
    reduce_scatter x1 -> x0, waiting for transfers between devices: 44.6 us -> none  [on_device(): lax.psum_scatter(terms.astype(jnp.bfloat16), 'ch', scatter_dimension=1, t...]
    all_to_all x2 -> x0, blocking collectives: 41.5 us -> none  [the longest x1 20.9 us: to_channels(): return lax.all_to_all(x, 'ctx', split_axis=0, concat_axis=0, tiled=True)]
    dot_general x1 -> x0, matrix products: 12.5 us -> none  [on_device(): terms = jnp.dot(gated, out_weight, preferred_element_type=jnp.float32)]
    all_to_all x1 -> x0, starting transfers between devices: 7.76 us -> none  [to_channels(): return lax.all_to_all(x, 'ctx', split_axis=0, concat_axis=0, tiled=True)]
    all_to_all x1 -> x0, waiting for transfers between devices: 5.83 us -> none  [to_channels(): return lax.all_to_all(x, 'ctx', split_axis=0, concat_axis=0, tiled=True)]
    ppermute x1 -> x0, starting transfers between devices: 4.94 us -> none  [passed_along(): return lax.ppermute(array, axis, pairs)]
    transpose x2 -> x0, local copies, waits for them, and re-layouts: 3.66 us -> none  [to_channels(): x = x.astype(jnp.bfloat16).T.reshape(count, chans // count, rows)]
  transfers between devices with their start and end apart: 3 -> 0, of which waited for: 2 -> 0; matrix products, arithmetic and copies ran while one was open for 7% -> 0% of each run, Pallas kernels for 0% -> 0%
where the time goes in v2:
time: 96 us; the launch traced here: 95.8 us
  Pallas kernels  93.5 us (97%)
  local copies, waits for them, and re-layouts  2.26 us (2%)
    pallas_call x1, Pallas kernels, on_device(): pl.pallas_call(functools.partial(kernel, blocks, ring), out_shape=jax.Sha...  93.5 us
    unnamed x1, local copies, waits for them, and re-layouts  2.26 us

profile of v2, /device:TPU:1, one launch (start us, length us, event | category | flops | bytes accessed | tf_op | source)
XLA Modules:
  0.0 95.8 jit_solution(14233422618486376412)
XLA Ops:
  0.0 93.5 %hyena_operator.1 = bf16[512,1024]{1,0:T(8,128)(2,1)} custom-call(bf16[3,512,1024]{2,1,0:T(8,128)(2,1)} %bitcast.2, f32[3,3,1024]{2,1,0:T(4,128)} %taps_ref.1, f32[512,1024]{1,0:T(8,128)} %filt_in.1, f32[1,1024]{1,0:T(1,128)} %bitcast.3, bf16[1024,4096]{1,0:T(8,128)(2,1)} %w_in.1, bf16[1024,512]{1,0:T(8,128)(2,1)} %constant.10.clone.first_in, ...), custom_call_target="tpu_custom_call" | custom-call | tf_op jit(solution)/shard_map/hyena_operator/pallas_call | solution.py:320
  93.5 2.3 %copy.12 = bf16[512,1024]{1,0:T(8,128)(2,1)} copy(bf16[512,1024]{1,0:T(8,128)(2,1)} %hyena_operator.1) | data formatting | bytes 2097152

commit v3 on v2

--- a/solution.py
+++ b/solution.py
@@ -64,8 +64,9 @@
     me = lax.axis_index("ctx")
     x = lax.axis_index("ch")
     _, rows, chans = br.shape
-    share = chans // blocks
-    groups = share // GROUP
+    groups = chans // blocks // GROUP
+    per = TILE // GROUP
+    owners = blocks // per
     half = blocks + 1
     quarters = rows // TILE
     right, left = lax.rem(x + 1, ring), lax.rem(x + ring - 1, ring)
@@ -77,7 +78,7 @@
             (square_in, square), (last_in, last), (w_in, w),
         ])
     ]
-    for copy in inputs:
+    for copy in inputs[:2]:
         copy.start()
 
     barrier = pltpu.get_barrier_semaphore()
@@ -93,11 +94,6 @@
 
     def lanes(i):
         return pl.ds(pl.multiple_of(i * TILE, TILE), TILE)
-
-    def turn_filter(i):
-        for r in range(quarters):
-            here = slice(r * TILE, (r + 1) * TILE)
-            h_send[lanes(i), here] = filt[here, lanes(i)].T.astype(jnp.bfloat16)
 
     def feature(r, i):
         here = slice(r * TILE, (r + 1) * TILE)
@@ -116,51 +112,66 @@
         driven = feats[1] * feats[2]
         query[here, lanes(i)] = feats[0]
         direct[here, lanes(i)] = skip_ref[:, lanes(i)] * driven
-        d_send[lanes(i), here] = driven.T.astype(jnp.bfloat16)
+        g, t = i // owners, lax.rem(i, owners) * per
+        d_send[g, pl.ds(t, per), :, here] = driven.T.astype(jnp.bfloat16).reshape(per, GROUP, TILE)
+
+    def ctx_copy(src, dst, send, recv, t):
+        return pltpu.make_async_remote_copy(
+            src_ref=src, dst_ref=dst, send_sem=send, recv_sem=recv,
+            device_id={"ctx": t}, device_id_type=MESH,
+        )
+
+    def scatter(src, dst, send, recv):
+        def one(k):
+            t = lax.rem(me + k, blocks)
+            ctx_copy(src(t), dst, send, recv, t).start()
+
+        loop(blocks, one, 1)
+        pltpu.make_async_copy(src(me), dst, recv).start()
+
+    def arrived(ref, sem):
+        pltpu.make_async_copy(ref, ref, sem).wait()
+
+    halo_copy = ctx_copy(
+        br_in.at[:, pl.ds(rows - GROUP, GROUP), :], halo, send_sem.at[0], halo_sem.at[0],
+        lax.rem(me + 1, blocks),
+    )
+
+    def turn_filter(k):
+        g, t = k // owners, lax.rem(me // per + k, owners)
+        i = g * owners + t
+        for r in range(quarters):
+            here = slice(r * TILE, (r + 1) * TILE)
+            turned_part = filt[here, lanes(i)].T.astype(jnp.bfloat16)
+            h_send[g, pl.ds(t * per, per), :, here] = turned_part.reshape(per, GROUP, TILE)
+
+        def one(j):
+            to = t * per + lax.rem(me + j, per)
+            src, dst = h_send.at[g, to], h_recv.at[g, me]
+
+            @pl.when(to == me)
+            def _():
+                pltpu.make_async_copy(src, dst, h_sem.at[g]).start()
+
+            @pl.when(to != me)
+            def _():
+                ctx_copy(src, dst, send_sem.at[1], h_sem.at[g], to).start()
+
+        loop(per, one)
 
     inputs[0].wait()
+    pl.semaphore_wait(barrier, blocks - 1 + 2)
+    halo_copy.start()
     loop(chans // TILE, turn_filter)
+    for copy in inputs[2:]:
+        copy.start()
     inputs[1].wait()
     for r in range(1, quarters):
         loop(chans // TILE, functools.partial(feature, r))
-
-    pl.semaphore_wait(barrier, blocks - 1 + 2)
-
-    halo_copy = pltpu.make_async_remote_copy(
-        src_ref=br.at[:, pl.ds(rows - GROUP, GROUP), :],
-        dst_ref=halo,
-        send_sem=send_sem.at[0],
-        recv_sem=halo_sem.at[0],
-        device_id={"ctx": lax.rem(me + 1, blocks)},
-        device_id_type=MESH,
-    )
-    halo_copy.start()
-
-    def scatter(src, dst, send, recv):
-        def one(k):
-            t = lax.rem(me + k, blocks)
-            pltpu.make_async_remote_copy(
-                src_ref=src(t), dst_ref=dst, send_sem=send, recv_sem=recv,
-                device_id={"ctx": t}, device_id_type=MESH,
-            ).start()
-
-        loop(blocks, one, 1)
-        pltpu.make_async_copy(src(me), dst, recv).start()
-
-    def block(t):
-        return pl.ds(pl.multiple_of(t * share, share), share)
-
-    def part_of(t, g):
-        return pl.ds(pl.multiple_of(t * share + g * GROUP, GROUP), GROUP)
-
-    scatter(lambda t: h_send.at[block(t)], h_recv.at[me], send_sem.at[1], h_sem.at[0])
     halo_copy.wait_recv()
     loop(chans // TILE, functools.partial(feature, 0))
     for g in range(groups):
-        scatter(lambda t: d_send.at[part_of(t, g)], d_recv.at[g, me], send_sem.at[2], d_sem.at[g])
-
-    def arrived(ref, sem):
-        pltpu.make_async_copy(ref, ref, sem).wait()
+        scatter(lambda t: d_send.at[g, t], d_recv.at[g, me], send_sem.at[2], d_sem.at[g])
 
     def forward(blocks_in, spec):
         col[...] = mul(first[...], blocks_in.reshape(blocks * GROUP, rows)).reshape(2 * blocks, GROUP, rows)
@@ -178,10 +189,10 @@
 
     for copy in inputs[2:7]:
         copy.wait()
-    arrived(h_recv, h_sem.at[0])
 
     def filter_group(g):
-        forward(h_recv[:, pl.ds(pl.multiple_of(g * GROUP, GROUP), GROUP), :], spec_h.at[g])
+        arrived(h_recv.at[g], h_sem.at[g])
+        forward(h_recv[g], spec_h.at[g])
 
     loop(groups, filter_group)
 
@@ -201,18 +212,16 @@
             wide[k] = (re * c - im * s).astype(jnp.bfloat16)
             if 0 < k < blocks:
                 wide[blocks + k] = (im * c + re * s).astype(jnp.bfloat16)
-        y = mul(last[...], wide[...].reshape(2 * blocks * GROUP, rows)).astype(jnp.bfloat16)
-        for q in range(quarters):
-            y_send[q, :, pl.ds(pl.multiple_of(g * GROUP, GROUP), GROUP), :] = y[
-                :, q * TILE:(q + 1) * TILE
-            ].reshape(blocks, GROUP, TILE)
+        for p in range(0, quarters, 2):
+            y = mul(last[...], wide[:, :, p * TILE:(p + 2) * TILE].reshape(2 * blocks * GROUP, 2 * TILE))
+            for q in (p, p + 1):
+                part = y[:, (q - p) * TILE:(q - p + 1) * TILE].astype(jnp.bfloat16)
+                y_send[q, g] = part.reshape(blocks, GROUP, TILE)
+                scatter(
+                    lambda t: y_send.at[q, g, t], y_recv.at[q, g, me], send_sem.at[3], y_sem.at[q, g]
+                )
 
     loop(groups, driven_group)
-
-    def give_back(q):
-        scatter(lambda t: y_send.at[q, t], y_recv.at[q, me], send_sem.at[3], y_sem.at[q])
-
-    loop(quarters, give_back)
     inputs[7].wait()
 
     def quarter(q):
@@ -229,11 +238,12 @@
         ).start()
 
     def opposite(q):
-        arrived(y_recv.at[q], y_sem.at[q])
+        for g in range(groups):
+            arrived(y_recv.at[q, g], y_sem.at[q, g])
 
         def gate(i):
-            per = TILE // share
-            turned_back = y_recv[q, pl.ds(i * per, per)].reshape(TILE, TILE).astype(jnp.float32).T
+            g, t = i // owners, lax.rem(i, owners) * per
+            turned_back = y_recv[q, g, pl.ds(t, per)].reshape(TILE, TILE).astype(jnp.float32).T
             value = query[quarter(q), lanes(i)] * (turned_back + direct[quarter(q), lanes(i)])
             gated[quarter(q), lanes(i)] = value.astype(jnp.bfloat16)
 
@@ -272,10 +282,9 @@
     loop(quarters, finish)
 
     halo_copy.wait_send()
-    arrived(h_send.at[pl.ds(0, chans - share)], send_sem.at[1])
-    arrived(d_send.at[pl.ds(0, chans - share)], send_sem.at[2])
-    others = y_send.at[:, pl.ds(0, blocks - 1)]
-    arrived(others, send_sem.at[3])
+    arrived(h_send.at[:, pl.ds(0, blocks - 1)], send_sem.at[1])
+    arrived(d_send.at[:, pl.ds(0, blocks - 1)], send_sem.at[2])
+    arrived(y_send.at[:, :, pl.ds(0, blocks - 1)], send_sem.at[3])
     arrived(s1, send_sem.at[4])
     arrived(s2, send_sem.at[5])
 
@@ -283,8 +292,7 @@
 def on_device(branches, short_kernel, long_filter, skip_gain, out_weight):
     blocks, ring = lax.axis_size("ctx"), lax.axis_size("ch")
     rows, _, chans = branches.shape
-    share, half, quarters = chans // blocks, blocks + 1, rows // TILE
-    groups = share // GROUP
+    half, quarters, groups = blocks + 1, rows // TILE, chans // blocks // GROUP
     bf16, f32 = jnp.bfloat16, jnp.float32
     consts = tables(blocks, rows)
     anywhere, vmem = pl.BlockSpec(memory_space=pl.ANY), pl.BlockSpec(memory_space=pltpu.VMEM)
@@ -295,12 +303,8 @@
         pltpu.VMEM(out_weight.shape, bf16),
         *[pltpu.VMEM(t.shape, t.dtype) for t in consts],
         pltpu.VMEM((3, GROUP, chans), bf16),
-        pltpu.VMEM((chans, rows), bf16),
-        pltpu.VMEM((chans, rows), bf16),
-        pltpu.VMEM((blocks, share, rows), bf16),
-        pltpu.VMEM((groups, blocks, GROUP, rows), bf16),
-        pltpu.VMEM((quarters, blocks, share, TILE), bf16),
-        pltpu.VMEM((quarters, blocks, share, TILE), bf16),
+        *[pltpu.VMEM((groups, blocks, GROUP, rows), bf16)] * 4,
+        *[pltpu.VMEM((quarters, groups, blocks, GROUP, TILE), bf16)] * 2,
         pltpu.VMEM((rows, chans), f32),
         pltpu.VMEM((rows, chans), f32),
         pltpu.VMEM((rows, chans), bf16),
@@ -314,12 +318,12 @@
         pltpu.VMEM((2, quarters, TILE // 2, chans), bf16),
         pltpu.VMEM((2, quarters, TILE, chans), bf16),
         pltpu.VMEM((2, quarters, TILE, chans), bf16),
-        dma((8,)), dma((1,)), dma((1,)), dma((groups,)), dma((quarters,)),
+        dma((8,)), dma((1,)), dma((groups,)), dma((groups,)), dma((quarters, groups)),
         dma((2, quarters)), dma((2, quarters)), dma((6,)),
     ]
     return pl.pallas_call(
         functools.partial(kernel, blocks, ring),
-        out_shape=jax.ShapeDtypeStruct((rows, chans), bf16),
+        out_shape=pltpu.VMEM((rows, chans), bf16),
         in_specs=[anywhere, vmem, anywhere, vmem] + [anywhere] * 6,
         out_specs=vmem,
         scratch_shapes=scratch,

time: 96 us -> 87.8 us (0.915)
  Pallas kernels: 93.5 us -> 86.7 us
  local copies, waits for them, and re-layouts: 2.26 us -> 0.97 us
    pallas_call x1, Pallas kernels: 93.5 us -> 86.7 us  [on_device(): pl.pallas_call(functools.partial(kernel, blocks, ring), out_shape=pltpu.V...]
    unnamed x1, local copies, waits for them, and re-layouts: 2.26 us -> 0.97 us
where the time goes in v3:
time: 87.8 us; the launch traced here: 87.6 us
  Pallas kernels  86.7 us (99%)
  local copies, waits for them, and re-layouts  0.97 us (1%)
    pallas_call x1, Pallas kernels, on_device(): pl.pallas_call(functools.partial(kernel, blocks, ring), out_shape=pltpu.V...  86.7 us

profile of v3, /device:TPU:1, one launch (start us, length us, event | category | flops | bytes accessed | tf_op | source)
XLA Modules:
  0.0 87.6 jit_solution(17451326348180678210)
XLA Ops:
  0.0 86.7 %hyena_operator.1 = bf16[512,1024]{1,0:T(8,128)(2,1)S(1)} custom-call(bf16[3,512,1024]{2,1,0:T(8,128)(2,1)} %bitcast.2, f32[3,3,1024]{2,1,0:T(4,128)} %taps_ref.1, f32[512,1024]{1,0:T(8,128)} %filt_in.1, f32[1,1024]{1,0:T(1,128)} %bitcast.3, bf16[1024,4096]{1,0:T(8,128)(2,1)} %w_in.1, bf16[1024,512]{1,0:T(8,128)(2,1)} %constant.10.clone.first_in, ...), custom_call_target="tpu_custom_call" | custom-call | tf_op jit(solution)/shard_map/hyena_operator/pallas_call | solution.py:324
  86.7 1.0 %copy.12 = bf16[512,1024]{1,0:T(8,128)(2,1)} copy(bf16[512,1024]{1,0:T(8,128)(2,1)S(1)} %hyena_operator.1) | data formatting | bytes 2097152

commit v4 on v3

--- a/solution.py
+++ b/solution.py
@@ -12,6 +12,8 @@
 MESH = pl.DeviceIdType.MESH
 GROUP = 16
 TILE = 128
+AHEAD = 2
+SHARED = 768
 
 
 def tables(blocks, rows):
@@ -58,8 +60,8 @@
     halo, h_send, d_send, h_recv, d_recv, y_send, y_recv,
     query, direct, gated, own,
     col, turned, spec_d, spec_h, wide,
-    s1, r1, s2, r2,
-    in_sem, halo_sem, h_sem, d_sem, y_sem, r1_sem, r2_sem, send_sem,
+    w_mate, gated_mate, pair_send, pair_recv, s1, r1, s2, r2,
+    in_sem, halo_sem, h_sem, d_sem, y_sem, w_sem, g_sem, p_sem, r1_sem, r2_sem, send_sem,
 ):
     me = lax.axis_index("ctx")
     x = lax.axis_index("ch")
@@ -69,7 +71,9 @@
     owners = blocks // per
     half = blocks + 1
     quarters = rows // TILE
-    right, left = lax.rem(x + 1, ring), lax.rem(x + ring - 1, ring)
+    right, left, across = lax.rem(x + 1, ring), lax.rem(x + ring - 1, ring), lax.rem(x + ring // 2, ring)
+    swap = lax.rem(x, 2) * lax.rem(me + 1, 2) + lax.rem(x + 1, 2) * lax.rem(me, 2)
+    mate, pair = right + swap * (left - right), left + swap * (right - left)
 
     inputs = [
         pltpu.make_async_copy(src, dst, in_sem.at[i])
@@ -129,6 +133,12 @@
         loop(blocks, one, 1)
         pltpu.make_async_copy(src(me), dst, recv).start()
 
+    def push(src, dst, send, recv, side):
+        pltpu.make_async_remote_copy(
+            src_ref=src, dst_ref=dst, send_sem=send, recv_sem=recv,
+            device_id={"ch": side}, device_id_type=MESH,
+        ).start()
+
     def arrived(ref, sem):
         pltpu.make_async_copy(ref, ref, sem).wait()
 
@@ -161,6 +171,11 @@
 
     inputs[0].wait()
     pl.semaphore_wait(barrier, blocks - 1 + 2)
+    for i, target in enumerate((mate, across)):
+        push(
+            w_in.at[:, pl.ds(pl.multiple_of(target * chans, chans), SHARED)], w_mate.at[i],
+            send_sem.at[6], w_sem.at[i], mate,
+        )
     halo_copy.start()
     loop(chans // TILE, turn_filter)
     for copy in inputs[2:]:
@@ -170,8 +185,11 @@
         loop(chans // TILE, functools.partial(feature, r))
     halo_copy.wait_recv()
     loop(chans // TILE, functools.partial(feature, 0))
-    for g in range(groups):
+    def send_driven(g):
         scatter(lambda t: d_send.at[g, t], d_recv.at[g, me], send_sem.at[2], d_sem.at[g])
+
+    arrived(h_send.at[:, pl.ds(0, blocks - 1)], send_sem.at[1])
+    send_driven(0)
 
     def forward(blocks_in, spec):
         col[...] = mul(first[...], blocks_in.reshape(blocks * GROUP, rows)).reshape(2 * blocks, GROUP, rows)
@@ -195,6 +213,9 @@
         forward(h_recv[g], spec_h.at[g])
 
     loop(groups, filter_group)
+    for g in range(1, groups):
+        arrived(d_send.at[g - 1, pl.ds(0, blocks - 1)], send_sem.at[2])
+        send_driven(g)
 
     def driven_group(g):
         arrived(d_recv.at[g], d_sem.at[g])
@@ -217,76 +238,98 @@
             for q in (p, p + 1):
                 part = y[:, (q - p) * TILE:(q - p + 1) * TILE].astype(jnp.bfloat16)
                 y_send[q, g] = part.reshape(blocks, GROUP, TILE)
-                scatter(
-                    lambda t: y_send.at[q, g, t], y_recv.at[q, g, me], send_sem.at[3], y_sem.at[q, g]
-                )
-
-    loop(groups, driven_group)
+
+    def give_back(q, g):
+        scatter(
+            lambda t: y_send.at[q, g, t], y_recv.at[q, g, me], send_sem.at[3], y_sem.at[q, g]
+        )
+
+    for g in range(groups):
+        driven_group(g)
+        loop(quarters, lambda q: give_back(q, g))
     inputs[7].wait()
 
     def quarter(q):
         return pl.ds(pl.multiple_of(q * TILE, TILE), TILE)
 
-    def project(q, target):
-        columns = pl.ds(pl.multiple_of(target * chans, chans), chans)
+    def project(q, target, start, width):
+        columns = pl.ds(pl.multiple_of(target * chans + start, TILE), width)
         return mul(gated[quarter(q)], w[:, columns])
 
-    def push(src, dst, send, recv, side):
-        pltpu.make_async_remote_copy(
-            src_ref=src, dst_ref=dst, send_sem=send, recv_sem=recv,
-            device_id={"ch": side}, device_id_type=MESH,
-        ).start()
+    apart = chans - SHARED
+
+    def gather(q, g):
+        arrived(y_recv.at[q, g], y_sem.at[q, g])
+
+        def gate(t):
+            i = g * owners + t
+            part = y_recv[q, g, pl.ds(t * per, per)].reshape(TILE, TILE).astype(jnp.float32).T
+            value = query[quarter(q), lanes(i)] * (part + direct[quarter(q), lanes(i)])
+            gated[quarter(q), lanes(i)] = value.astype(jnp.bfloat16)
+
+        loop(owners, gate)
+        here = (quarter(q), slice(g * owners * TILE, (g + 1) * owners * TILE))
+        push(gated.at[here], gated_mate.at[here], send_sem.at[7], g_sem.at[q, g], mate)
 
     def opposite(q):
-        for g in range(groups):
-            arrived(y_recv.at[q, g], y_sem.at[q, g])
-
-        def gate(i):
-            g, t = i // owners, lax.rem(i, owners) * per
-            turned_back = y_recv[q, g, pl.ds(t, per)].reshape(TILE, TILE).astype(jnp.float32).T
-            value = query[quarter(q), lanes(i)] * (turned_back + direct[quarter(q), lanes(i)])
-            gated[quarter(q), lanes(i)] = value.astype(jnp.bfloat16)
-
-        loop(chans // TILE, gate)
-        terms = project(q, lax.rem(x + 2, ring)).astype(jnp.bfloat16)
+        gather(q, groups - 1)
+        terms = project(q, across, SHARED, apart).astype(jnp.bfloat16)
         s1[0, q] = terms[:TILE // 2]
         s1[1, q] = terms[TILE // 2:]
         push(s1.at[0, q], r1.at[0, q], send_sem.at[4], r1_sem.at[0, q], right)
         push(s1.at[1, q], r1.at[1, q], send_sem.at[4], r1_sem.at[1, q], left)
 
     def beside(q):
+        for g in range(groups):
+            here = (quarter(q), slice(g * owners * TILE, (g + 1) * owners * TILE))
+            arrived(gated_mate.at[here], g_sem.at[q, g])
+        theirs = gated_mate[quarter(q)]
+        terms = project(q, pair, 0, SHARED) + mul(theirs, w_mate[1])
+        pair_send[quarter(q)] = terms.astype(jnp.bfloat16)
+        push(pair_send.at[quarter(q)], pair_recv.at[quarter(q)], send_sem.at[8], p_sem.at[q], pair)
         for side, (target, lo, hi) in enumerate([(right, 0, TILE // 2), (left, TILE // 2, TILE)]):
-            terms = project(q, target)
+            terms = project(q, target, SHARED, apart)
             arrived(r1.at[side, q], r1_sem.at[side, q])
             s2[side, q, lo:hi] = (terms[lo:hi] + r1[side, q].astype(jnp.float32)).astype(jnp.bfloat16)
             other = slice(TILE // 2 - lo, TILE + TILE // 2 - hi)
             s2[side, q, other] = terms[other].astype(jnp.bfloat16)
             push(s2.at[side, q], r2.at[side, q], send_sem.at[5], r2_sem.at[side, q], target)
-        own[quarter(q)] = project(q, x)
-
-    opposite(0)
+        own[quarter(q), :SHARED] = project(q, x, 0, SHARED) + mul(theirs, w_mate[0])
+        own[quarter(q), SHARED:] = project(q, x, SHARED, apart)
+
+    for g in range(groups - 1):
+        loop(quarters, lambda q: gather(q, g))
+    loop(AHEAD, opposite)
+    for i in range(2):
+        arrived(w_mate.at[i], w_sem.at[i])
 
     def steady(q):
-        opposite(q + 1)
+        opposite(q + AHEAD)
         beside(q)
 
-    loop(quarters - 1, steady)
-    beside(quarters - 1)
+    if AHEAD < quarters:
+        loop(quarters - AHEAD, steady)
+    loop(quarters, beside, quarters - AHEAD)
 
     def finish(q):
+        arrived(pair_recv.at[quarter(q)], p_sem.at[q])
+        total = own[quarter(q), :SHARED] + pair_recv[quarter(q)].astype(jnp.float32)
+        out_ref[quarter(q), :SHARED] = total.astype(out_ref.dtype)
         for side in range(2):
             arrived(r2.at[side, q], r2_sem.at[side, q])
-        total = own[quarter(q)] + r2[0, q].astype(jnp.float32) + r2[1, q].astype(jnp.float32)
-        out_ref[quarter(q)] = total.astype(out_ref.dtype)
+        total = own[quarter(q), SHARED:] + r2[0, q].astype(jnp.float32) + r2[1, q].astype(jnp.float32)
+        out_ref[quarter(q), SHARED:] = total.astype(out_ref.dtype)
 
     loop(quarters, finish)
 
     halo_copy.wait_send()
-    arrived(h_send.at[:, pl.ds(0, blocks - 1)], send_sem.at[1])
-    arrived(d_send.at[:, pl.ds(0, blocks - 1)], send_sem.at[2])
+    arrived(d_send.at[groups - 1, pl.ds(0, blocks - 1)], send_sem.at[2])
     arrived(y_send.at[:, :, pl.ds(0, blocks - 1)], send_sem.at[3])
     arrived(s1, send_sem.at[4])
     arrived(s2, send_sem.at[5])
+    arrived(w_mate, send_sem.at[6])
+    arrived(gated, send_sem.at[7])
+    arrived(pair_send, send_sem.at[8])
 
 
 def on_device(branches, short_kernel, long_filter, skip_gain, out_weight):
@@ -314,12 +357,13 @@
         pltpu.VMEM((half * GROUP, 2 * rows), f32),
         pltpu.VMEM((groups, half * GROUP, 2 * rows), f32),
         pltpu.VMEM((2 * blocks, GROUP, rows), bf16),
-        pltpu.VMEM((2, quarters, TILE // 2, chans), bf16),
-        pltpu.VMEM((2, quarters, TILE // 2, chans), bf16),
-        pltpu.VMEM((2, quarters, TILE, chans), bf16),
-        pltpu.VMEM((2, quarters, TILE, chans), bf16),
+        pltpu.VMEM((2, chans, SHARED), bf16),
+        pltpu.VMEM((rows, chans), bf16),
+        *[pltpu.VMEM((rows, SHARED), bf16)] * 2,
+        *[pltpu.VMEM((2, quarters, TILE // 2, chans - SHARED), bf16)] * 2,
+        *[pltpu.VMEM((2, quarters, TILE, chans - SHARED), bf16)] * 2,
         dma((8,)), dma((1,)), dma((groups,)), dma((groups,)), dma((quarters, groups)),
-        dma((2, quarters)), dma((2, quarters)), dma((6,)),
+        dma((2,)), dma((quarters, groups)), dma((quarters,)), dma((2, quarters)), dma((2, quarters)), dma((9,)),
     ]
     return pl.pallas_call(
         functools.partial(kernel, blocks, ring),

time: 87.8 us -> 75.3 us (0.86)
  Pallas kernels: 86.7 us -> 74.2 us
    pallas_call x1, Pallas kernels: 86.7 us -> 74.2 us  [on_device(): pl.pallas_call(functools.partial(kernel, blocks, ring), out_shape=pltpu.V...]
where the time goes in v4:
time: 75.3 us; the launch traced here: 75.2 us
  Pallas kernels  74.2 us (99%)
  local copies, waits for them, and re-layouts  0.97 us (1%)
    pallas_call x1, Pallas kernels, on_device(): pl.pallas_call(functools.partial(kernel, blocks, ring), out_shape=pltpu.V...  74.2 us

profile of v4, /device:TPU:1, one launch (start us, length us, event | category | flops | bytes accessed | tf_op | source)
XLA Modules:
  0.0 75.2 jit_solution(6731817259980640674)
XLA Ops:
  0.0 74.2 %hyena_operator.1 = bf16[512,1024]{1,0:T(8,128)(2,1)S(1)} custom-call(bf16[3,512,1024]{2,1,0:T(8,128)(2,1)} %bitcast.2, f32[3,3,1024]{2,1,0:T(4,128)} %taps_ref.1, f32[512,1024]{1,0:T(8,128)} %filt_in.1, f32[1,1024]{1,0:T(1,128)} %bitcast.3, bf16[1024,4096]{1,0:T(8,128)(2,1)} %w_in.1, bf16[1024,512]{1,0:T(8,128)(2,1)} %constant.10.clone.first_in, ...), custom_call_target="tpu_custom_call" | custom-call | tf_op jit(solution)/shard_map/hyena_operator/pallas_call | solution.py:368
  74.2 1.0 %copy.12 = bf16[512,1024]{1,0:T(8,128)(2,1)} copy(bf16[512,1024]{1,0:T(8,128)(2,1)S(1)} %hyena_operator.1) | data formatting | bytes 2097152

commit v5 on v4

--- a/solution.py
+++ b/solution.py
@@ -12,6 +12,9 @@
 MESH = pl.DeviceIdType.MESH
 GROUP = 16
 TILE = 128
+STRIDE = 13
+SPREAD = 7
+INVERSE = 23
 AHEAD = 2
 SHARED = 768
 
@@ -54,9 +57,9 @@
 
 def kernel(
     blocks, ring,
-    br_in, taps_ref, filt_in, skip_ref, w_in, first_in, last_in, square_in, cos_in, sin_in,
+    br_in, taps_in, filt_in, skip_in, w_in, first_in, last_in, square_in, cos_in, sin_in,
     out_ref,
-    br, filt, w, first, last, square, tw_cos, tw_sin,
+    br, filt, w, first, last, square, tw_cos, tw_sin, taps_ref, skip_ref,
     halo, h_send, d_send, h_recv, d_recv, y_send, y_recv,
     query, direct, gated, own,
     col, turned, spec_d, spec_h, wide,
@@ -78,11 +81,11 @@
     inputs = [
         pltpu.make_async_copy(src, dst, in_sem.at[i])
         for i, (src, dst) in enumerate([
-            (filt_in, filt), (br_in, br), (first_in, first), (cos_in, tw_cos), (sin_in, tw_sin),
+            (filt_in, filt), (taps_in, taps_ref), (skip_in, skip_ref), (br_in, br), (first_in, first), (cos_in, tw_cos), (sin_in, tw_sin),
             (square_in, square), (last_in, last), (w_in, w),
         ])
     ]
-    for copy in inputs[:2]:
+    for copy in inputs[:4]:
         copy.start()
 
     barrier = pltpu.get_barrier_semaphore()
@@ -92,9 +95,9 @@
             barrier, inc=1, device_id={"ctx": lax.rem(me + k, blocks)}, device_id_type=MESH
         )
 
-    loop(blocks, greet, 1)
     for side in (left, right):
         pl.semaphore_signal(barrier, inc=1, device_id={"ch": side}, device_id_type=MESH)
+    loop(blocks, greet, 1)
 
     def lanes(i):
         return pl.ds(pl.multiple_of(i * TILE, TILE), TILE)
@@ -125,9 +128,12 @@
             device_id={"ctx": t}, device_id_type=MESH,
         )
 
+    def place(t):
+        return lax.rem(t * INVERSE, blocks)
+
     def scatter(src, dst, send, recv):
         def one(k):
-            t = lax.rem(me + k, blocks)
+            t = lax.rem(me + k * STRIDE, blocks)
             ctx_copy(src(t), dst, send, recv, t).start()
 
         loop(blocks, one, 1)
@@ -156,8 +162,9 @@
             h_send[g, pl.ds(t * per, per), :, here] = turned_part.reshape(per, GROUP, TILE)
 
         def one(j):
-            to = t * per + lax.rem(me + j, per)
-            src, dst = h_send.at[g, to], h_recv.at[g, me]
+            here = t * per + lax.rem(me + j, per)
+            to = lax.rem(here * SPREAD, blocks)
+            src, dst = h_send.at[g, here], h_recv.at[g, me]
 
             @pl.when(to == me)
             def _():
@@ -169,7 +176,6 @@
 
         loop(per, one)
 
-    inputs[0].wait()
     pl.semaphore_wait(barrier, blocks - 1 + 2)
     for i, target in enumerate((mate, across)):
         push(
@@ -177,16 +183,18 @@
             send_sem.at[6], w_sem.at[i], mate,
         )
     halo_copy.start()
+    inputs[0].wait()
     loop(chans // TILE, turn_filter)
-    for copy in inputs[2:]:
+    for copy in inputs[4:]:
         copy.start()
-    inputs[1].wait()
+    for copy in inputs[1:4]:
+        copy.wait()
     for r in range(1, quarters):
         loop(chans // TILE, functools.partial(feature, r))
     halo_copy.wait_recv()
     loop(chans // TILE, functools.partial(feature, 0))
     def send_driven(g):
-        scatter(lambda t: d_send.at[g, t], d_recv.at[g, me], send_sem.at[2], d_sem.at[g])
+        scatter(lambda t: d_send.at[g, place(t)], d_recv.at[g, me], send_sem.at[2], d_sem.at[g])
 
     arrived(h_send.at[:, pl.ds(0, blocks - 1)], send_sem.at[1])
     send_driven(0)
@@ -205,7 +213,7 @@
             turned[k, :, rows:] = b.astype(jnp.bfloat16)
         spec[...] = mul(turned[...].reshape(half * GROUP, 2 * rows), square[...])
 
-    for copy in inputs[2:7]:
+    for copy in inputs[4:9]:
         copy.wait()
 
     def filter_group(g):
@@ -241,13 +249,13 @@
 
     def give_back(q, g):
         scatter(
-            lambda t: y_send.at[q, g, t], y_recv.at[q, g, me], send_sem.at[3], y_sem.at[q, g]
+            lambda t: y_send.at[q, g, t], y_recv.at[q, g, place(me)], send_sem.at[3], y_sem.at[q, g]
         )
 
     for g in range(groups):
         driven_group(g)
         loop(quarters, lambda q: give_back(q, g))
-    inputs[7].wait()
+    inputs[9].wait()
 
     def quarter(q):
         return pl.ds(pl.multiple_of(q * TILE, TILE), TILE)
@@ -345,6 +353,8 @@
         pltpu.VMEM((rows, chans), f32),
         pltpu.VMEM(out_weight.shape, bf16),
         *[pltpu.VMEM(t.shape, t.dtype) for t in consts],
+        pltpu.VMEM(short_kernel.shape, f32),
+        pltpu.VMEM((1, chans), f32),
         pltpu.VMEM((3, GROUP, chans), bf16),
         *[pltpu.VMEM((groups, blocks, GROUP, rows), bf16)] * 4,
         *[pltpu.VMEM((quarters, groups, blocks, GROUP, TILE), bf16)] * 2,
@@ -362,13 +372,13 @@
         *[pltpu.VMEM((rows, SHARED), bf16)] * 2,
         *[pltpu.VMEM((2, quarters, TILE // 2, chans - SHARED), bf16)] * 2,
         *[pltpu.VMEM((2, quarters, TILE, chans - SHARED), bf16)] * 2,
-        dma((8,)), dma((1,)), dma((groups,)), dma((groups,)), dma((quarters, groups)),
+        dma((10,)), dma((1,)), dma((groups,)), dma((groups,)), dma((quarters, groups)),
         dma((2,)), dma((quarters, groups)), dma((quarters,)), dma((2, quarters)), dma((2, quarters)), dma((9,)),
     ]
     return pl.pallas_call(
         functools.partial(kernel, blocks, ring),
         out_shape=pltpu.VMEM((rows, chans), bf16),
-        in_specs=[anywhere, vmem, anywhere, vmem] + [anywhere] * 6,
+        in_specs=[anywhere] * 10,
         out_specs=vmem,
         scratch_shapes=scratch,
         compiler_params=pltpu.CompilerParams(

time: 75.3 us -> 74.6 us (level)
  no operation moved by 1% of the time
where the time goes in v5:
time: 74.6 us; the launch traced here: 74.5 us
  Pallas kernels  73.5 us (99%)
  local copies, waits for them, and re-layouts  0.97 us (1%)
    pallas_call x1, Pallas kernels, on_device(): pl.pallas_call(functools.partial(kernel, blocks, ring), out_shape=pltpu.V...  73.5 us

profile of v5, /device:TPU:1, one launch (start us, length us, event | category | flops | bytes accessed | tf_op | source)
XLA Modules:
  0.0 74.5 jit_solution(6100767404058252453)
XLA Ops:
  0.0 73.5 %hyena_operator.1 = bf16[512,1024]{1,0:T(8,128)(2,1)S(1)} custom-call(bf16[3,512,1024]{2,1,0:T(8,128)(2,1)} %bitcast.2, f32[3,3,1024]{2,1,0:T(4,128)} %taps_in.1, f32[512,1024]{1,0:T(8,128)} %filt_in.1, f32[1,1024]{1,0:T(1,128)} %bitcast.3, bf16[1024,4096]{1,0:T(8,128)(2,1)} %w_in.1, bf16[1024,512]{1,0:T(8,128)(2,1)} %constant.10.clone.first_in, ...), custom_call_target="tpu_custom_call" | custom-call | tf_op jit(solution)/shard_map/hyena_operator/pallas_call | solution.py:378
  73.5 1.0 %copy.12 = bf16[512,1024]{1,0:T(8,128)(2,1)} copy(bf16[512,1024]{1,0:T(8,128)(2,1)S(1)} %hyena_operator.1) | data formatting | bytes 2097152

commit v6 on v5

--- a/solution.py
+++ b/solution.py
@@ -177,7 +177,7 @@
         loop(per, one)
 
     pl.semaphore_wait(barrier, blocks - 1 + 2)
-    for i, target in enumerate((mate, across)):
+    for i, target in ((1, across), (0, mate)):
         push(
             w_in.at[:, pl.ds(pl.multiple_of(target * chans, chans), SHARED)], w_mate.at[i],
             send_sem.at[6], w_sem.at[i], mate,
@@ -302,14 +302,18 @@
             other = slice(TILE // 2 - lo, TILE + TILE // 2 - hi)
             s2[side, q, other] = terms[other].astype(jnp.bfloat16)
             push(s2.at[side, q], r2.at[side, q], send_sem.at[5], r2_sem.at[side, q], target)
+
+        @pl.when(q == 0)
+        def _():
+            arrived(w_mate.at[0], w_sem.at[0])
+
         own[quarter(q), :SHARED] = project(q, x, 0, SHARED) + mul(theirs, w_mate[0])
         own[quarter(q), SHARED:] = project(q, x, SHARED, apart)
 
     for g in range(groups - 1):
         loop(quarters, lambda q: gather(q, g))
     loop(AHEAD, opposite)
-    for i in range(2):
-        arrived(w_mate.at[i], w_sem.at[i])
+    arrived(w_mate.at[1], w_sem.at[1])
 
     def steady(q):
         opposite(q + AHEAD)

time: 74.6 us -> 74.6 us (level)
  no operation moved by 1% of the time
where the time goes in v6:
time: 74.6 us; the launch traced here: 74.5 us
  Pallas kernels  73.5 us (99%)
  local copies, waits for them, and re-layouts  0.97 us (1%)
    pallas_call x1, Pallas kernels, on_device(): pl.pallas_call(functools.partial(kernel, blocks, ring), out_shape=pltpu.V...  73.5 us

profile of v6, /device:TPU:1, one launch (start us, length us, event | category | flops | bytes accessed | tf_op | source)
XLA Modules:
  0.0 74.5 jit_solution(3891038383149914576)
XLA Ops:
  0.0 73.5 %hyena_operator.1 = bf16[512,1024]{1,0:T(8,128)(2,1)S(1)} custom-call(bf16[3,512,1024]{2,1,0:T(8,128)(2,1)} %bitcast.2, f32[3,3,1024]{2,1,0:T(4,128)} %taps_in.1, f32[512,1024]{1,0:T(8,128)} %filt_in.1, f32[1,1024]{1,0:T(1,128)} %bitcast.3, bf16[1024,4096]{1,0:T(8,128)(2,1)} %w_in.1, bf16[1024,512]{1,0:T(8,128)(2,1)} %constant.10.clone.first_in, ...), custom_call_target="tpu_custom_call" | custom-call | tf_op jit(solution)/shard_map/hyena_operator/pallas_call | solution.py:382
  73.5 1.0 %copy.12 = bf16[512,1024]{1,0:T(8,128)(2,1)} copy(bf16[512,1024]{1,0:T(8,128)(2,1)S(1)} %hyena_operator.1) | data formatting | bytes 2097152
